TPU v7x, 128 devices: a whole 4x4x4 slice. The times are simulated.
128 devices in a mesh: band: 4 (over z), tile: 32 (over x, y, core).
Axes of the slice: x: 4, y: 4, z: 4, core: 2. Of those that a mesh axis runs over, the one named last changes fastest.
Arguments:
- increment: float32 [64, 5, 256, 768], P('band', None, 'tile'), may hold values from -6 to 6
- courant_x: float32 [64, 256, 768], P('band', 'tile'), may hold values from -0.45 to 0.45
- courant_y: float32 [64, 256, 768], P('band', 'tile'), may hold values from -0.45 to 0.45
- level_inverse: float32 [5, 64, 16], P(None, 'band'), may hold values from -0.25 to 1.25, as said below
- coupling: float32 [5], replicated, may hold values from 0.5 to 2
- profile: float32 [64, 5, 64], P('band'), may hold values from -0.3125 to 0.3125
- send_column: int32 [32, 8192], P('tile'), may hold values from 0 to 6143
- send_block: int32 [32, 8192], P('tile'), may hold values from 0 to 63
- send_count: int32 [32, 32], P('tile'), may hold values from 1 to 256, as said below
- obs_weight: float32 [32, 8192], P('tile'), may hold values from 1 to 10
Outputs:
- hessian: float32 [64, 5, 256, 768], P('band', None, 'tile')
Inputs may be any that keep to these rules, and one draw needn't show every extreme that they name: `level_inverse`: rows b * 16 to b * 16 + 15 of each variable hold the block of band b. `send_column`: column index within the sending tile's own rows. Row t, column d: the slots k < send_count[t, d] of the group sent from tile t to owner d are live; in every draw some owner receives 256 from every tile.
All inputs are finite; a program needn't handle non-finite values.
Results may differ from a plain program's by a relative error of at most 0.0001.
Values sent between devices are 32-bit elements; how exact they have to be, the bound alone decides.
A program may use at most 64 MiB of HBM per device.

v0:
```python
import functools

import jax
import jax.numpy as jnp
from jax import lax
from jax.experimental import pallas as pl
from jax.experimental.pallas import tpu as pltpu
from jax.sharding import PartitionSpec as P

MESH = pl.DeviceIdType.MESH
VARS = 5
LEVB = 16
LV = VARS * LEVB
ROWS = 8
NX = 768
BANDS = 4
TILES = 32
CHUNK = 256
CHUNKS = 32
WIDE = 256
WINDOWS = 24
PAIRS = 56
NBLK = 64
ORDER = (1, 2, 3, 4, 5, 6, 0, 7)
SPLIT = 24
F32 = jnp.float32
BF16 = jnp.bfloat16


def halves(value):
    high = value.astype(BF16)
    low = (value - high.astype(F32)).astype(BF16)
    return high, low


def mm(a, b):
    return jnp.dot(a, b, preferred_element_type=F32)


def kernel(
    inc_ref, cx_ref, cy_ref, mats_ref, cols_ref, coef_ref, prof_ref, cell_ref, blk_ref, wgt_ref, pair_ref,
    out_ref,
    field, cyh, co, adj, local, stack, mext, edges, recv, coefs, ps, xs, onehot, val, valr, acc,
    halo_s, halo_r, cy_s, cy_r, cf_s, cf_r, ed_s, ed_r, va_s, va_r,
):
    band = lax.axis_index("band")
    tile = lax.axis_index("tile")
    north = lax.rem(tile + 1, TILES)
    south = lax.rem(tile + TILES - 1, TILES)
    partner = [lax.rem(band + o, BANDS) for o in (1, 2, 3)]

    barrier = pltpu.get_barrier_semaphore()
    for t in (north, south):
        pl.semaphore_signal(barrier, inc=1, device_id={"tile": t}, device_id_type=MESH)
    for p in partner:
        pl.semaphore_signal(barrier, inc=1, device_id={"band": p}, device_id_type=MESH)
    pl.semaphore_wait(barrier, 5)

    sent = []

    def halo(buffer, send, receive):
        up = pltpu.make_async_remote_copy(
            buffer.at[ROWS], buffer.at[0], send.at[0], receive.at[0],
            device_id={"tile": north}, device_id_type=MESH)
        down = pltpu.make_async_remote_copy(
            buffer.at[1], buffer.at[ROWS + 1], send.at[1], receive.at[1],
            device_id={"tile": south}, device_id_type=MESH)
        up.start()
        down.start()
        sent.extend([up, down])
        return up, down

    def band_copy(source, target, send, receive, o):
        copy = pltpu.make_async_remote_copy(
            source, target, send, receive, device_id={"band": partner[o]}, device_id_type=MESH)
        copy.start()
        sent.append(copy)
        return copy

    for v in range(VARS):
        turned = jnp.swapaxes(inc_ref[:, v], 0, 1)
        field[0, 1:ROWS + 1, LEVB * v:LEVB * v + LEVB, :] = turned
    halo1 = halo(field.at[0], halo_s.at[0], halo_r.at[0])
    coefs[0] = coef_ref[...]
    cf_copies = [
        band_copy(coefs.at[0], coefs.at[o + 1], cf_s.at[o], cf_r.at[o], o) for o in range(3)
    ]
    cyh[1:ROWS + 1] = jnp.swapaxes(cy_ref[...], 0, 1)
    halo_cy = halo(cyh, cy_s, cy_r)
    co[0] = jnp.swapaxes(cx_ref[...], 0, 1)

    lane = lax.broadcasted_iota(jnp.int32, (LEVB, NX), 1)
    for y in range(ROWS):
        cx = co[0, y]
        cy = cyh[y + 1]
        ax, bx = (jnp.abs(cx) + cx) * 0.5, (jnp.abs(cx) - cx) * 0.5
        ay, by = (jnp.abs(cy) + cy) * 0.5, (jnp.abs(cy) - cy) * 0.5
        co[0, y] = 1.0 - ax - bx - ay - by
        co[1, y] = jnp.where(lane == 0, 0.0, ax)
        co[2, y] = jnp.where(lane == NX - 1, 0.0, bx)
        if y == 0:
            ay = jnp.where(tile == 0, 0.0, ay)
        if y == ROWS - 1:
            by = jnp.where(tile == TILES - 1, 0.0, by)
        co[3, y] = ay
        co[4, y] = by
        adj[0, y] = jnp.where(lane == 0, 0.0, pltpu.roll(bx, 1, 1))
        adj[1, y] = jnp.where(lane == NX - 1, 0.0, pltpu.roll(ax, NX - 1, 1))

    profiles = jnp.concatenate(halves(prof_ref[...]), axis=0)
    block_iota = lax.broadcasted_iota(jnp.int32, (NBLK, CHUNK), 0)

    def pick_profiles(c, carry):
        hot = (block_iota == blk_ref[c]).astype(BF16)
        picked = mm(profiles, hot)
        ps[c] = picked[:LV] + picked[LV:]
        return carry

    lax.fori_loop(0, CHUNKS, pick_profiles, 0)

    for copy in cf_copies:
        copy.wait_recv()

    def of_band(lane_index):
        result = []
        for j in range(BANDS):
            total = jnp.zeros((8, 1), F32)
            for b in range(BANDS):
                entry = coefs[(b - j) % BANDS][:, lane_index:lane_index + 1]
                total = total + jnp.where(band == b, entry, 0.0)
            result.append(total)
        return result

    def select(values):
        total = jnp.zeros((8, 1), F32)
        for b in range(BANDS):
            total = total + jnp.where(band == b, values[b], 0.0)
        return total

    k0, k15, g0 = of_band(0), of_band(1), of_band(2)
    zero = jnp.zeros((8, 1), F32)

    def chain(a, g):
        e = [zero] * (BANDS + 1)
        for j in range(BANDS - 1, -1, -1):
            e[j] = k0[j] + g[j] * e[j + 1] * a[j]
        into_first = select([g[b] * e[b + 1] for b in range(BANDS)])
        own = select([e[b + 1] for b in range(BANDS)])
        low, high = [], []
        for o in (1, 2, 3):
            t_list, s_list = [], []
            for b in range(BANDS):
                j = (b - o) % BANDS
                factor = zero + 1.0
                if j < b:
                    for k in range(j + 1, b):
                        factor = factor * a[k]
                    t_list.append(factor)
                    s_list.append(e[b + 1] * a[b] * factor)
                else:
                    for k in range(b + 1, j):
                        factor = factor * g[k]
                    t_list.append(zero)
                    s_list.append(factor)
            low.append(select(t_list))
            high.append(select(s_list))
        return into_first, own, low, high

    chains = (chain(k15, g0), chain(g0, k15))
    for kind in range(2):
        matrix = mats_ref[kind]
        last = matrix[LV:LV + 8]
        first = matrix[LV + 8:LV + 16] + chains[kind][0] * last
        matrix = jnp.concatenate([matrix[:LV + 8], first], axis=0)
        high, low = halves(matrix)
        mext[kind, 0] = high
        mext[kind, 1] = low

    def stencil(src, y, v, kind):
        rows = slice(LEVB * v, LEVB * v + LEVB)
        f = field[src, y + 1, rows, :]
        west, east = pltpu.roll(f, 1, 1), pltpu.roll(f, NX - 1, 1)
        if kind == 0:
            cw, ce, cs, cn = (co[i, y] for i in (1, 2, 3, 4))
        else:
            cw, ce, cs, cn = adj[0, y], adj[1, y], adj[2, y], adj[3, y]
        return (
            co[0, y] * f + cw * west + ce * east
            + cs * field[src, y, rows, :] + cn * field[src, y + 2, rows, :]
        )

    def solve(stage, kind, row_value, before_last, store_row, after_edges):
        copies = []
        for k, y in enumerate(ORDER):
            if k == 6:
                before_last()
            for v in range(VARS):
                high, low = halves(row_value(y, v))
                rows = slice(LEVB * v, LEVB * v + LEVB)
                stack[k % 2, 0, rows, :] = high
                stack[k % 2, 1, rows, :] = low
            high, low = stack[k % 2, 0], stack[k % 2, 1]
            lhs = jnp.concatenate([mext[kind, 0], mext[kind, 1]], axis=0)
            first = mm(lhs, high)
            result = first[:LV + 16] + first[LV + 16:] + mm(mext[kind, 0], low)
            local[y] = result[:LV]
            edges[stage, 0, VARS * k:VARS * k + VARS, :] = result[LV:LV + VARS]
            edges[stage, 1, VARS * k:VARS * k + VARS, :] = result[LV + 8:LV + 8 + VARS]
            for part, (at, lo, hi) in enumerate(((4, 0, SPLIT), (7, SPLIT, VARS * ROWS))):
                if k == at:
                    for o in range(3):
                        above = (band + o + 1) // BANDS
                        copies.append(band_copy(
                            edges.at[stage, above, lo:hi], recv.at[stage, o, lo:hi],
                            ed_s.at[stage, o, part], ed_r.at[stage, o, part], o))
        for copy in copies:
            copy.wait_recv()
        _, own, low_c, high_c = chains[kind]
        left, right = cols_ref[kind, :, 0:1], cols_ref[kind, :, 1:2]
        for y in (0, 7, 1, 2, 3, 4, 5, 6):
            k = ORDER.index(y)
            span = slice(VARS * k, VARS * k + VARS)
            t = jnp.zeros((VARS, NX), F32)
            s = own[:VARS] * edges[stage, 0, span, :]
            for o in range(3):
                got = recv[stage, o, span, :]
                t = t + low_c[o][:VARS] * got
                s = s + high_c[o][:VARS] * got
            for v in range(VARS):
                rows = slice(LEVB * v, LEVB * v + LEVB)
                store_row(y, v, local[y, rows, :] + left[rows] * t[v:v + 1] + right[rows] * s[v:v + 1])
            if y == 7:
                after_edges()

    pending = {}

    def wait_halo(copies):
        for copy in copies:
            copy.wait_recv()

    def into_field(index):
        def store(y, v, value):
            field[index, y + 1, LEVB * v:LEVB * v + LEVB, :] = value
        return store

    def send_field(index):
        def send():
            pending[index] = halo(field.at[index], halo_s.at[index], halo_r.at[index])
        return send

    def store_state(y, v, value):
        high, low = halves(value)
        for j in range(3):
            cols = slice(WIDE * j, WIDE * j + WIDE)
            xs[3 * y + j, LEVB * v:LEVB * v + LEVB, :] = high[:, cols]
            xs[3 * y + j, LV + LEVB * v:LV + LEVB * v + LEVB, :] = low[:, cols]

    solve(0, 0, lambda y, v: stencil(0, y, v, 0), lambda: wait_halo(halo1), into_field(1), send_field(1))
    solve(1, 0, lambda y, v: stencil(1, y, v, 0), lambda: wait_halo(pending[1]), store_state, lambda: None)

    cell_iota = lax.broadcasted_iota(jnp.int32, (WIDE, CHUNK), 0)

    def observe(p, carry):
        c, w, base = pair_ref[0, p], pair_ref[1, p], pair_ref[2, p]
        hot = (cell_iota == cell_ref[c] - base).astype(BF16)
        onehot[p] = hot
        picked = mm(xs[w], hot)
        product = (picked[:LV] + picked[LV:]) * ps[c]
        val[p] = jnp.sum(product, axis=0, keepdims=True)
        return carry

    lax.fori_loop(0, PAIRS, observe, 0)
    copies = [band_copy(val, valr.at[o], va_s.at[o], va_r.at[o], o) for o in range(3)]

    wait_halo(halo_cy)
    for y in range(ROWS):
        below, above = cyh[y], cyh[y + 2]
        by = (jnp.abs(below) - below) * 0.5
        ay = (jnp.abs(above) + above) * 0.5
        if y == 0:
            by = jnp.where(tile == 0, 0.0, by)
        if y == ROWS - 1:
            ay = jnp.where(tile == TILES - 1, 0.0, ay)
        adj[2, y] = by
        adj[3, y] = ay
    for copy in copies:
        copy.wait_recv()

    def spread(p, before):
        c, same = pair_ref[0, p], pair_ref[3, p]
        values = (val[p] + valr[0, p]) + (valr[1, p] + valr[2, p])
        high, low = halves(ps[c] * (values * wgt_ref[c]))
        both = jnp.concatenate([high, low], axis=0)
        added = lax.dot_general(both, onehot[p], (((1,), (1,)), ((), ())), preferred_element_type=F32)
        total = before * same.astype(F32) + (added[:LV] + added[LV:])
        acc[p] = total
        return total

    lax.fori_loop(0, PAIRS, spread, jnp.zeros((LV, WIDE), F32))

    def gradient(y, v):
        parts = []
        for j in range(3):
            w = 3 * y + j
            some = pair_ref[5, w].astype(F32)
            parts.append(acc[pair_ref[4, w], LEVB * v:LEVB * v + LEVB, :] * some)
        return jnp.concatenate(parts, axis=1)

    solve(2, 1, gradient, lambda: None, into_field(2), send_field(2))
    solve(3, 1, lambda y, v: stencil(2, y, v, 1), lambda: wait_halo(pending[2]), into_field(3), send_field(3))

    for k, y in enumerate(ORDER):
        if k == 6:
            wait_halo(pending[3])
        for v in range(VARS):
            result = stencil(3, y, v, 1) + field[0, y + 1, LEVB * v:LEVB * v + LEVB, :]
            local[y, LEVB * v:LEVB * v + LEVB, :] = result
    for v in range(VARS):
        out_ref[:, v] = jnp.swapaxes(local[:, LEVB * v:LEVB * v + LEVB, :], 0, 1)
    for copy in sent:
        copy.wait_send()


def block_diagonal(blocks):
    eye = jnp.eye(VARS, dtype=F32)
    return (eye[:, None, :, None] * blocks[:, :, None, :]).reshape(VARS * blocks.shape[1], -1)


def shards(
    increment, courant_x, courant_y, level_inverse, coupling, profile, send_column, send_block, send_count, obs_weight,
):
    inverse = level_inverse
    scale = coupling[:, None]
    pad3 = jnp.zeros((3, LV), F32)

    def extended(main, last, first):
        return jnp.concatenate(
            [block_diagonal(main), block_diagonal(last[:, None]), pad3, block_diagonal(first[:, None]), pad3])

    first_column, last_column = scale * inverse[:, :, 0], scale * inverse[:, :, LEVB - 1]
    mats = jnp.stack([
        extended(inverse, inverse[:, LEVB - 1], inverse[:, 0]),
        extended(inverse.transpose(0, 2, 1), last_column, first_column),
    ])
    cols = jnp.stack([
        jnp.stack([first_column.reshape(LV), last_column.reshape(LV)], axis=1),
        jnp.stack([inverse[:, 0].reshape(LV), inverse[:, LEVB - 1].reshape(LV)], axis=1),
    ])
    cols = jnp.pad(cols, ((0, 0), (0, 0), (0, 126)))
    coef = jnp.stack([first_column[:, 0], first_column[:, LEVB - 1], last_column[:, 0]], axis=1)
    coef = jnp.pad(coef, ((0, 3), (0, 125)))
    table = profile.transpose(1, 0, 2).reshape(LV, NBLK)

    weight = lax.all_to_all(obs_weight.reshape(TILES, -1), "tile", split_axis=0, concat_axis=0, tiled=True)
    slot = lax.broadcasted_iota(jnp.int32, weight.shape, 1)
    weight = jnp.where(slot < send_count.reshape(TILES)[:, None], weight, 0.0)
    key = send_column[0] * NBLK + send_block[0]
    key, weight = lax.sort((key, weight.reshape(-1)), num_keys=1)
    cell, blk = (key // NBLK).reshape(CHUNKS, CHUNK), (key % NBLK).reshape(CHUNKS, CHUNK)
    weight = weight.reshape(CHUNKS, CHUNK)
    first, last = cell[:, 0] // WIDE, cell[:, CHUNK - 1] // WIDE
    number = last - first + 1
    order = jnp.arange(CHUNKS)
    start = jnp.sum(jnp.where(order[None, :] < order[:, None], number[None, :], 0), axis=1)
    p = jnp.arange(64)
    chunk = jnp.sum((start[None, :] <= p[:, None]).astype(jnp.int32), axis=1) - 1
    mine = chunk[:, None] == order[None, :]
    window = jnp.sum(jnp.where(mine, first[None, :] - start[None, :], 0), axis=1) + p
    valid = p < jnp.sum(number)
    window_index = jnp.where(valid, window, WINDOWS - 1)
    base = jnp.where(valid, window * WIDE, -(1 << 20))
    same = jnp.concatenate([jnp.zeros((1,), jnp.int32), (window_index[1:] == window_index[:-1]).astype(jnp.int32)])
    hit = (p[:, None] == window_index[None, :]) & valid[None, :]
    latest = jnp.max(jnp.where(hit, p[None, :], 0), axis=1)
    some = jnp.max(hit.astype(jnp.int32), axis=1)
    pairs = jnp.stack([chunk, window_index, base, same, latest, some]).astype(jnp.int32)

    vmem = pl.BlockSpec(memory_space=pltpu.VMEM)
    dma = pltpu.SemaphoreType.DMA
    out = pl.pallas_call(
        kernel,
        out_shape=jax.ShapeDtypeStruct(increment.shape, F32),
        in_specs=[vmem] * 10 + [pl.BlockSpec(memory_space=pltpu.SMEM)],
        out_specs=vmem,
        scratch_shapes=[
            pltpu.VMEM((4, ROWS + 2, LV, NX), F32),
            pltpu.VMEM((ROWS + 2, LEVB, NX), F32),
            pltpu.VMEM((5, ROWS, LEVB, NX), F32),
            pltpu.VMEM((4, ROWS, LEVB, NX), F32),
            pltpu.VMEM((ROWS, LV, NX), F32),
            pltpu.VMEM((2, 2, LV, NX), BF16),
            pltpu.VMEM((2, 2, LV + 16, LV), BF16),
            pltpu.VMEM((4, 2, VARS * ROWS, NX), F32),
            pltpu.VMEM((4, 3, VARS * ROWS, NX), F32),
            pltpu.VMEM((4, 8, 128), F32),
            pltpu.VMEM((CHUNKS, LV, CHUNK), F32),
            pltpu.VMEM((WINDOWS, 2 * LV, WIDE), BF16),
            pltpu.VMEM((PAIRS, WIDE, CHUNK), BF16),
            pltpu.VMEM((PAIRS, 1, CHUNK), F32),
            pltpu.VMEM((3, PAIRS, 1, CHUNK), F32),
            pltpu.VMEM((PAIRS, LV, WIDE), F32),
            dma((4, 2)), dma((4, 2)), dma((2,)), dma((2,)), dma((3,)), dma((3,)),
            dma((4, 3, 2)), dma((4, 3, 2)), dma((3,)), dma((3,)),
        ],
        compiler_params=pltpu.CompilerParams(
            collective_id=0, has_side_effects=True, vmem_limit_bytes=56 * 1024 * 1024),
    )(
        increment, courant_x, courant_y, mats, cols, coef, table,
        cell.reshape(CHUNKS, 1, CHUNK), blk.reshape(CHUNKS, 1, CHUNK), weight.reshape(CHUNKS, 1, CHUNK), pairs,
    )
    return out


def solution(mesh):
    return jax.shard_map(
        shards,
        mesh=mesh,
        in_specs=(
            P("band", None, "tile", None),
            P("band", "tile", None),
            P("band", "tile", None),
            P(None, "band", None),
            P(),
            P("band", None, None),
            P("tile", None),
            P("tile", None),
            P("tile", None),
            P("tile", None),
        ),
        out_specs=P("band", None, "tile", None),
        check_vma=False,
    )
```

profile of v0, /device:TPU:0, one launch (start us, length us, event | category | flops | bytes accessed | tf_op | source)
XLA Modules:
  0.0 121.6 jit_solution(16619907200739252974)
XLA Ops:
  0.0 7.5 %all-to-all-start = ((f32[32,1,256]{2,1,0:T(1,128)}), f32[32,1,256]{2,1,0:T(1,128)S(1)}, u32[]{:S(2)}, u32[]{:S(2)}) async-start(f32[32,1,256]{2,1,0:T(1,128)} %bitcast.54), calls=%async_computation | async-start | bytes 65536 | tf_op jit(solution)/shard_map/all_to_all | solution.py:354
  7.6 0.9 fusion.9
  8.5 0.1 copy.59
  8.7 0.1 copy.58
  8.8 0.1 squeeze.21
  8.9 0.7 bitcast_multiply_fusion
  9.6 0.7 mul.194
  10.4 0.7 iota_compare_fusion.1
  11.2 0.5 broadcast.249
  11.7 1.4 %fusion.7 = (f32[5,16]{1,0:T(8,128)S(1)}, f32[5,1,16]{2,1,0:T(1,128)S(1)}, f32[5,16]{1,0:T(8,128)S(1)}, f32[5,1,16]{2,1,0:T(1,128)S(1)}) fusion(f32[]{:T(128)} %broadcast.249, f32[5,16,16]{2,1,0:T(8,128)} %param.13), kind=kLoop, calls=%fused_computation.63 | loop fusion | bytes 1924 | tf_op jit(solution)/shard_map/slice | solution.py:342
  13.2 0.9 copy.52
  14.5 0.9 broadcast_multiply_fusion.1
  15.4 0.1 mul.181
  15.6 0.1 mul.193
  15.9 0.7 pad_maximum_fusion.mats_ref
  16.5 0.7 select_maximum_fusion.coef_ref
  17.2 0.1 copy.55
  17.3 0.6 pad.8.cols_ref
  18.0 6.9 %sort.23 = (s32[8192]{0:T(1024)S(1)}, f32[8192]{0:T(1024)}, s32[8192]{0:T(1024)}) sort(s32[8192]{0:T(1024)S(1)} %bitcast.49, f32[8192]{0:T(1024)S(1)} %broadcast_select_fusion, s32[8192]{0:T(1024)S(1)} %iota.92), dimensions={0}, to_apply=%region_0.1 | sort | flops 106496 | bytes 196608 | tf_op jit(solution)/shard_map/sort | solution.py:358
  24.9 0.6 add_select_fusion
  25.6 0.2 slice_reduce_fusion.1
  25.7 0.7 fusion.6
  26.5 0.1 select_reduce_fusion.2
  26.6 0.1 convert_reduce_fusion.1
  26.7 0.7 iota_compare_fusion.8
  27.4 0.1 select_reduce_fusion.1
  27.5 0.7 add_select_fusion.2
  28.2 0.7 compare_select_fusion.6
  29.0 0.1 convert_reduce_fusion
  29.2 0.6 stack.58.pair_ref
  29.8 88.9 %shard_map.100 = f32[16,5,8,768]{3,2,1,0:T(8,128)} custom-call(f32[16,5,8,768]{3,2,1,0:T(8,128)} %inc_ref.1, f32[16,8,768]{2,1,0:T(8,128)} %cx_ref.1, f32[16,8,768]{2,1,0:T(8,128)} %cy_ref.1, f32[2,96,80]{2,1,0:T(8,128)} %pad_maximum_fusion.mats_ref, f32[2,80,128]{2,1,0:T(8,128)} %pad.8.cols_ref, f32[8,128]{1,0:T(8,128)} %select_maximum_fusion.coef_ref, ...), custom_call_target="tpu_custom_call" | custom-call | tf_op jit(solution)/shard_map/pallas_call | solution.py:380
  118.7 2.9 %copy.63 = f32[16,5,8,768]{3,2,1,0:T(8,128)} copy(f32[16,5,8,768]{3,2,1,0:T(8,128)} %shard_map.100) | data formatting | bytes 3932160
  (34 shorter events, 1.1 us)
Async XLA Ops:
  0.0 15.7 %copy-start.1 = (s32[1,8192]{1,0:T(1,128)S(1)}, s32[1,8192]{1,0:T(1,128)}, u32[]{:S(2)}) copy-start(s32[1,8192]{1,0:T(1,128)} %param.17) | copy-start | bytes 98308
  0.0 15.7 %copy-start.2 = (s32[1,8192]{1,0:T(1,128)S(1)}, s32[1,8192]{1,0:T(1,128)}, u32[]{:S(2)}) copy-start(s32[1,8192]{1,0:T(1,128)} %param.16) | copy-start | bytes 98308
  0.0 18.0 %all-to-all-start = ((f32[32,1,256]{2,1,0:T(1,128)}), f32[32,1,256]{2,1,0:T(1,128)S(1)}, u32[]{:S(2)}, u32[]{:S(2)}) async-start(f32[32,1,256]{2,1,0:T(1,128)} %bitcast.54), calls=%async_computation | async-start | bytes 65536 | tf_op jit(solution)/shard_map/all_to_all | solution.py:354
  25.6 4.2 %copy-start = (s32[8192]{0:T(1024)}, s32[8192]{0:T(1024)S(1)}, u32[]{:S(2)}) copy-start(s32[8192]{0:T(1024)S(1)} %get-tuple-element.27) | copy-start | bytes 98308
where the time goes:
time: 122 us
  Pallas kernels  88.9 us (73%)
  other arithmetic  14.8 us (12%)
  local copies, waits for them, and re-layouts  10.3 us (8%)
  starting transfers between devices  7.53 us (6%)
    pallas_call x1, Pallas kernels, shards(): pl.pallas_call(kernel, out_shape=jax.ShapeDtypeStruct(increment.shape, F3...  88.9 us
    all_to_all x1, starting transfers between devices, shards(): lax.all_to_all(obs_weight.reshape(TILES, -1), 'tile', split_axis=0, conca...  7.53 us
    sort x1, other arithmetic, shards(): key, weight = lax.sort((key, weight.reshape(-1)), num_keys=1)  6.92 us
    unnamed x9, local copies, waits for them, and re-layouts  3.18 us
  transfers between devices with their start and end apart: 1, of which 0 were waited for; matrix products, arithmetic and copies ran while one was open for 8% of the time, Pallas kernels for 0%

commit v1 on v0

v1 whole, which is shorter than its diff:
```python
import functools

import jax
import jax.numpy as jnp
from jax import lax
from jax.experimental import pallas as pl
from jax.experimental.pallas import tpu as pltpu
from jax.sharding import PartitionSpec as P

MESH = pl.DeviceIdType.MESH
VARS = 5
LEVB = 16
LV = VARS * LEVB
ROWS = 8
NX = 768
BANDS = 4
TILES = 32
CHUNK = 256
CHUNKS = 32
WIDE = 256
WINDOWS = 24
PAIRS = 56
NBLK = 64
ORDER = (1, 2, 3, 4, 5, 6, 0, 7)
SPLIT = 24
F32 = jnp.float32
BF16 = jnp.bfloat16


def halves(value):
    high = value.astype(BF16)
    low = (value - high.astype(F32)).astype(BF16)
    return high, low


def mm(a, b):
    return jnp.dot(a, b, preferred_element_type=F32)


def wide(value):
    return jnp.concatenate([value] * (NX // 128), axis=1)


def sort_pairs(keys, payload):
    shape = keys.shape
    slab, sub, lane = (lax.broadcasted_iota(jnp.int32, shape, axis) for axis in range(3))
    place = lane * 64 + sub * 8 + slab
    for k in range(1, 14):
        for j in range(k - 1, -1, -1):
            distance = 1 << j
            bit, block = (place >> j) & 1, (place >> k) & 1
            flip = bit != block
            if j < 3:
                def partner(x):
                    parts = x.reshape(8 >> (j + 1), 2, distance, 8, 128)
                    return jnp.concatenate([parts[:, 1:], parts[:, :1]], axis=1).reshape(shape)
            else:
                axis, step, size = (1, distance >> 3, 8) if j < 6 else (2, distance >> 6, 128)

                def partner(x):
                    if 2 * step == size:
                        return pltpu.roll(x, step, axis)
                    return jnp.where(bit == 1, pltpu.roll(x, step, axis), pltpu.roll(x, size - step, axis))
            other, other_payload = partner(keys), partner(payload)
            take = jnp.where(flip, (keys < other).astype(jnp.int32), (keys > other).astype(jnp.int32)) == 1
            keys = jnp.where(take, other, keys)
            payload = jnp.where(take, other_payload, payload)
    return keys, payload


def kernel(
    inc_ref, cx_ref, cy_ref, inv_ref, prof_ref, column_ref, block_ref, weight_ref, coupling_ref, count_ref,
    out_ref,
    field, cyh, co, adj, local, stack, mext, gm, cols, tab, edges, recv, coefs, wbuf, wrow, turn, turn_key, keyr, wgtr, pairv,
    ps, xs, onehot, val, valr, acc, finals, pair_ref,
    halo_s, halo_r, cy_s, cy_r, cf_s, cf_r, ed_s, ed_r, va_s, va_r, wt_s, wt_r, pair_sem, out_sem,
):
    band = lax.axis_index("band")
    tile = lax.axis_index("tile")
    north = lax.rem(tile + 1, TILES)
    south = lax.rem(tile + TILES - 1, TILES)
    partner = [lax.rem(band + o, BANDS) for o in (1, 2, 3)]

    barrier = pltpu.get_barrier_semaphore()
    for o in range(1, TILES):
        pl.semaphore_signal(
            barrier, inc=1, device_id={"tile": lax.rem(tile + o, TILES)}, device_id_type=MESH)
    for p in partner:
        pl.semaphore_signal(barrier, inc=1, device_id={"band": p}, device_id_type=MESH)
    pl.semaphore_wait(barrier, TILES + BANDS - 2)

    sent = []

    def halo(buffer, send, receive):
        up = pltpu.make_async_remote_copy(
            buffer.at[ROWS], buffer.at[0], send.at[0], receive.at[0],
            device_id={"tile": north}, device_id_type=MESH)
        down = pltpu.make_async_remote_copy(
            buffer.at[1], buffer.at[ROWS + 1], send.at[1], receive.at[1],
            device_id={"tile": south}, device_id_type=MESH)
        up.start()
        down.start()
        sent.extend([up, down])
        return up, down

    def band_copy(source, target, send, receive, o):
        copy = pltpu.make_async_remote_copy(
            source, target, send, receive, device_id={"band": partner[o]}, device_id_type=MESH)
        copy.start()
        sent.append(copy)
        return copy

    for v in range(VARS):
        turned = jnp.swapaxes(inc_ref[:, v], 0, 1)
        field[0, 1:ROWS + 1, LEVB * v:LEVB * v + LEVB, :] = turned
    halo1 = halo(field.at[0], halo_s.at[0], halo_r.at[0])
    gm[...] = jnp.zeros((2, 128, 128), F32)
    for v in range(VARS):
        rows = slice(LEVB * v, LEVB * v + LEVB)
        gm[0, rows, rows] = inv_ref[v]
        tab[rows, :] = prof_ref[:, v, :]
    gm[1] = gm[0].T
    row_lane = lax.broadcasted_iota(jnp.int32, (8, 128), 1)

    def at_lanes(offset, factors):
        total = jnp.zeros((8, 128), F32)
        for v in range(VARS):
            total = total + jnp.where(row_lane == LEVB * v + offset, factors[v], 0.0)
        return total

    def rows_of(kind, offset):
        rows = [gm[kind, LEVB * v + offset:LEVB * v + offset + 1, :] for v in range(VARS)]
        if kind == 1:
            rows = [coupling_ref[v] * rows[v] for v in range(VARS)]
        return jnp.concatenate(rows + [jnp.zeros((3, 128), F32)], axis=0)

    ones = [1.0] * VARS
    scales = [coupling_ref[v] for v in range(VARS)]
    scale_first, scale_last = at_lanes(0, scales), at_lanes(LEVB - 1, scales)
    one_first, one_last = at_lanes(0, ones), at_lanes(LEVB - 1, ones)
    lasts = [rows_of(kind, LEVB - 1) for kind in range(2)]
    firsts = [rows_of(kind, 0) for kind in range(2)]

    def across(value, weight):
        return jnp.broadcast_to(jnp.sum(value * weight[0:1], axis=1, keepdims=True), (value.shape[0], 128))

    coefs[0, 0] = across(firsts[0], scale_first)
    coefs[0, 1] = across(lasts[0], scale_first)
    coefs[0, 2] = across(firsts[0], scale_last)
    cf_copies = [
        band_copy(coefs.at[0], coefs.at[o + 1], cf_s.at[o], cf_r.at[o], o) for o in range(3)
    ]
    cols[0, 0] = across(gm[0, :LV], scale_first)
    cols[0, 1] = across(gm[0, :LV], scale_last)
    cols[1, 0] = across(gm[1, :LV], one_first)
    cols[1, 1] = across(gm[1, :LV], one_last)

    wt_copies = []
    for o in range(1, TILES):
        target = lax.rem(tile + o, TILES)
        copy = pltpu.make_async_remote_copy(
            weight_ref.at[pl.ds(2 * target, 2)], wbuf.at[pl.ds(2 * tile, 2)], wt_s.at[o - 1], wt_r.at[o - 1],
            device_id={"tile": target}, device_id_type=MESH)
        copy.start()
        sent.append(copy)
        wt_copies.append(copy)
    cyh[1:ROWS + 1] = jnp.swapaxes(cy_ref[...], 0, 1)
    halo_cy = halo(cyh, cy_s, cy_r)
    co[0] = jnp.swapaxes(cx_ref[...], 0, 1)

    lane = lax.broadcasted_iota(jnp.int32, (LEVB, NX), 1)
    for y in range(ROWS):
        cx = co[0, y]
        cy = cyh[y + 1]
        ax, bx = (jnp.abs(cx) + cx) * 0.5, (jnp.abs(cx) - cx) * 0.5
        ay, by = (jnp.abs(cy) + cy) * 0.5, (jnp.abs(cy) - cy) * 0.5
        co[0, y] = 1.0 - ax - bx - ay - by
        co[1, y] = jnp.where(lane == 0, 0.0, ax)
        co[2, y] = jnp.where(lane == NX - 1, 0.0, bx)
        if y == 0:
            ay = jnp.where(tile == 0, 0.0, ay)
        if y == ROWS - 1:
            by = jnp.where(tile == TILES - 1, 0.0, by)
        co[3, y] = ay
        co[4, y] = by
        adj[0, y] = jnp.where(lane == 0, 0.0, pltpu.roll(bx, 1, 1))
        adj[1, y] = jnp.where(lane == NX - 1, 0.0, pltpu.roll(ax, NX - 1, 1))

    for copy in cf_copies:
        copy.wait_recv()

    def of_band(lane_index):
        result = []
        for j in range(BANDS):
            total = jnp.zeros((8, 128), F32)
            for b in range(BANDS):
                entry = coefs[(b - j) % BANDS, lane_index]
                total = total + jnp.where(band == b, entry, 0.0)
            result.append(total)
        return result

    def select(values):
        total = jnp.zeros((8, 128), F32)
        for b in range(BANDS):
            total = total + jnp.where(band == b, values[b], 0.0)
        return total

    k0, k15, g0 = of_band(0), of_band(1), of_band(2)
    zero = jnp.zeros((8, 128), F32)

    def chain(a, g):
        e = [zero] * (BANDS + 1)
        for j in range(BANDS - 1, -1, -1):
            e[j] = k0[j] + g[j] * e[j + 1] * a[j]
        into_first = select([g[b] * e[b + 1] for b in range(BANDS)])
        own = select([e[b + 1] for b in range(BANDS)])
        low, high = [], []
        for o in (1, 2, 3):
            t_list, s_list = [], []
            for b in range(BANDS):
                j = (b - o) % BANDS
                factor = zero + 1.0
                if j < b:
                    for k in range(j + 1, b):
                        factor = factor * a[k]
                    t_list.append(factor)
                    s_list.append(e[b + 1] * a[b] * factor)
                else:
                    for k in range(b + 1, j):
                        factor = factor * g[k]
                    t_list.append(zero)
                    s_list.append(factor)
            low.append(select(t_list))
            high.append(select(s_list))
        return into_first, own, low, high

    chains = (chain(k15, g0), chain(g0, k15))
    for kind in range(2):
        first = firsts[kind] + chains[kind][0] * lasts[kind]
        matrix = jnp.concatenate([gm[kind, :LV, :], lasts[kind], first], axis=0)[:, :LV]
        high, low = halves(matrix)
        mext[kind] = jnp.concatenate([high, high, low], axis=1)

    def stencil(src, y, v, kind):
        rows = slice(LEVB * v, LEVB * v + LEVB)
        f = field[src, y + 1, rows, :]
        west, east = pltpu.roll(f, 1, 1), pltpu.roll(f, NX - 1, 1)
        if kind == 0:
            cw, ce, cs, cn = (co[i, y] for i in (1, 2, 3, 4))
        else:
            cw, ce, cs, cn = adj[0, y], adj[1, y], adj[2, y], adj[3, y]
        return (
            co[0, y] * f + cw * west + ce * east
            + cs * field[src, y, rows, :] + cn * field[src, y + 2, rows, :]
        )

    def solve(stage, kind, row_value, before_last, store_row, after_edges, gap=None):
        copies = []
        for k, y in enumerate(ORDER):
            if k == 6:
                before_last()
            for v in range(VARS):
                high, low = halves(row_value(y, v))
                rows = slice(LEVB * v, LEVB * v + LEVB)
                stack[k % 2, rows, :] = high
                stack[k % 2, LV + LEVB * v:LV + LEVB * v + LEVB, :] = low
                stack[k % 2, 2 * LV + LEVB * v:2 * LV + LEVB * v + LEVB, :] = high
            result = mm(mext[kind], stack[k % 2])
            local[y] = result[:LV]
            edges[stage, 0, VARS * k:VARS * k + VARS, :] = result[LV:LV + VARS]
            edges[stage, 1, VARS * k:VARS * k + VARS, :] = result[LV + 8:LV + 8 + VARS]
            for part, (at, lo, hi) in enumerate(((4, 0, SPLIT), (7, SPLIT, VARS * ROWS))):
                if k == at:
                    for o in range(3):
                        above = (band + o + 1) // BANDS
                        copies.append(band_copy(
                            edges.at[stage, above, lo:hi], recv.at[stage, o, lo:hi],
                            ed_s.at[stage, o, part], ed_r.at[stage, o, part], o))
        if gap is not None:
            gap()
        for copy in copies:
            copy.wait_recv()
        _, own, low_c, high_c = chains[kind]
        for y in (0, 7, 1, 2, 3, 4, 5, 6):
            k = ORDER.index(y)
            span = slice(VARS * k, VARS * k + VARS)
            t = jnp.zeros((VARS, NX), F32)
            s = wide(own[:VARS]) * edges[stage, 0, span, :]
            for o in range(3):
                got = recv[stage, o, span, :]
                t = t + wide(low_c[o][:VARS]) * got
                s = s + wide(high_c[o][:VARS]) * got
            for v in range(VARS):
                rows = slice(LEVB * v, LEVB * v + LEVB)
                left, right = wide(cols[kind, 0, rows, :]), wide(cols[kind, 1, rows, :])
                store_row(y, v, local[y, rows, :] + left * t[v:v + 1] + right * s[v:v + 1])
            if y == 7:
                after_edges()

    pending = {}

    def wait_halo(copies):
        for copy in copies:
            copy.wait_recv()

    def into_field(index):
        def store(y, v, value):
            field[index, y + 1, LEVB * v:LEVB * v + LEVB, :] = value
        return store

    def send_field(index):
        def send():
            pending[index] = halo(field.at[index], halo_s.at[index], halo_r.at[index])
        return send

    def store_state(y, v, value):
        high, low = halves(value)
        for j in range(3):
            cols = slice(WIDE * j, WIDE * j + WIDE)
            xs[3 * y + j, LEVB * v:LEVB * v + LEVB, :] = high[:, cols]
            xs[3 * y + j, LV + LEVB * v:LV + LEVB * v + LEVB, :] = low[:, cols]

    def sort_slots():
        for copy in wt_copies:
            copy.wait_recv()
        own = pl.ds(2 * tile, 2)
        wbuf[own] = weight_ref[own]
        slot = lax.broadcasted_iota(jnp.int32, (1, 128), 1)
        for r in range(64):
            live = slot < count_ref[0, r // 2] - 128 * (r % 2)
            wrow[r:r + 1, :] = jnp.where(live, wbuf[r], 0.0)
        keys = (column_ref[...] * NBLK + block_ref[...]).reshape(8, 8, 128)
        keys, weights = sort_pairs(keys, wrow[...].reshape(8, 8, 128))
        turn_key[0:64, :] = keys.reshape(64, 128)
        turn_key[64:128, :] = jnp.zeros((64, 128), jnp.int32)
        turn_key[...] = turn_key[...].T
        turn[0:64, :] = weights.reshape(64, 128)
        turn[64:128, :] = jnp.zeros((64, 128), F32)
        turn[...] = turn[...].T

        def rows_of_chunks(ref):
            return jnp.concatenate(
                [ref[pl.ds(q, CHUNKS, stride=4), :][:, :64] for q in range(4)], axis=1)

        rows, weights = rows_of_chunks(turn_key), rows_of_chunks(turn)
        for c in range(CHUNKS):
            keyr[c] = rows[c:c + 1]
            wgtr[c] = weights[c:c + 1]
        first = jnp.broadcast_to(rows[:, 0:1] // (NBLK * WIDE), (CHUNKS, 128))
        last = jnp.broadcast_to(rows[:, CHUNK - 1:CHUNK] // (NBLK * WIDE), (CHUNKS, 128))
        number = last - first + 1
        sub = lax.broadcasted_iota(jnp.int32, (CHUNKS, 128), 0)
        p = lax.broadcasted_iota(jnp.int32, (CHUNKS, 128), 1)
        upto = number
        for d in (1, 2, 4, 8, 16):
            upto = upto + jnp.where(sub >= d, pltpu.roll(upto, d, 0), 0)
        start = upto - number

        def down(value):
            return jnp.sum(value, axis=0, keepdims=True)

        chunk = jnp.clip(down(jnp.where(start <= p, 1, 0)) - 1, 0, CHUNKS - 1)
        window = down(jnp.where(sub == chunk, first - start + p, 0))
        valid = p[0:1] < upto[CHUNKS - 1:CHUNKS]
        index = jnp.clip(jnp.where(valid, window, WINDOWS - 1), 0, WINDOWS - 1)
        base = jnp.where(valid, window * WIDE, -(1 << 20))
        same = jnp.where((p[0:1] > 0) & (index == pltpu.roll(index, 1, 1)), 1, 0)
        latest = jnp.clip(down(jnp.clip(p - first + 1, 0, number)) - 1, 0, PAIRS - 1)
        some = jnp.minimum(down(jnp.where((first <= p) & (p <= last), 1, 0)), 1)
        zeros = jnp.zeros((2, 128), jnp.int32)
        pairv[...] = jnp.concatenate([chunk, index, base, same, latest, some, zeros], axis=0)
        copy = pltpu.make_async_copy(pairv, pair_ref, pair_sem)
        copy.start()
        copy.wait()

    def pick_slots():
        profiles = jnp.concatenate(halves(tab[...]), axis=0)
        block_iota = lax.broadcasted_iota(jnp.int32, (NBLK, CHUNK), 0)
        cell_iota = lax.broadcasted_iota(jnp.int32, (WIDE, CHUNK), 0)

        def pick_profiles(i, carry):
            for u in range(4):
                c = 4 * i + u
                picked = mm(profiles, (block_iota == keyr[c] % NBLK).astype(BF16))
                ps[c] = picked[:LV] + picked[LV:]
            return carry

        lax.fori_loop(0, CHUNKS // 4, pick_profiles, 0)

        def pick_cells(i, carry):
            for u in range(4):
                p = 4 * i + u
                onehot[p] = (cell_iota == keyr[pair_ref[0, p]] // NBLK - pair_ref[2, p]).astype(BF16)
            return carry

        lax.fori_loop(0, PAIRS // 4, pick_cells, 0)

    solve(0, 0, lambda y, v: stencil(0, y, v, 0), lambda: wait_halo(halo1), into_field(1), send_field(1), sort_slots)
    solve(1, 0, lambda y, v: stencil(1, y, v, 0), lambda: wait_halo(pending[1]), store_state, lambda: None, pick_slots)

    def observe(i, carry):
        for u in range(4):
            p = 4 * i + u
            picked = mm(xs[pair_ref[1, p]], onehot[p])
            product = (picked[:LV] + picked[LV:]) * ps[pair_ref[0, p]]
            val[p] = jnp.sum(product, axis=0, keepdims=True)
        return carry

    lax.fori_loop(0, PAIRS // 4, observe, 0)
    copies = [band_copy(val, valr.at[o], va_s.at[o], va_r.at[o], o) for o in range(3)]

    wait_halo(halo_cy)
    for y in range(ROWS):
        below, above = cyh[y], cyh[y + 2]
        by = (jnp.abs(below) - below) * 0.5
        ay = (jnp.abs(above) + above) * 0.5
        if y == 0:
            by = jnp.where(tile == 0, 0.0, by)
        if y == ROWS - 1:
            ay = jnp.where(tile == TILES - 1, 0.0, ay)
        adj[2, y] = by
        adj[3, y] = ay
    for copy in copies:
        copy.wait_recv()

    def spread(i, before):
        for u in range(4):
            p = 4 * i + u
            c = pair_ref[0, p]
            values = (val[p] + valr[0, p]) + (valr[1, p] + valr[2, p])
            high, low = halves(ps[c] * (values * wgtr[c]))
            both = jnp.concatenate([high, low], axis=0)
            added = lax.dot_general(
                both, onehot[p], (((1,), (1,)), ((), ())), preferred_element_type=F32)
            before = before * pair_ref[3, p].astype(F32) + (added[:LV] + added[LV:])
            acc[p] = before
        return before

    lax.fori_loop(0, PAIRS // 4, spread, jnp.zeros((LV, WIDE), F32))

    def gradient(y, v):
        parts = []
        for j in range(3):
            w = 3 * y + j
            some = pair_ref[5, w].astype(F32)
            parts.append(acc[pair_ref[4, w], LEVB * v:LEVB * v + LEVB, :] * some)
        return jnp.concatenate(parts, axis=1)

    solve(2, 1, gradient, lambda: None, into_field(2), send_field(2))
    solve(3, 1, lambda y, v: stencil(2, y, v, 1), lambda: wait_halo(pending[2]), into_field(3), send_field(3))

    def finish(y, v):
        rows = slice(LEVB * v, LEVB * v + LEVB)
        local[y, rows, :] = stencil(3, y, v, 1) + field[0, y + 1, rows, :]

    for y in ORDER[:6]:
        for v in range(VARS):
            finish(y, v)
    wait_halo(pending[3])
    outs = []
    for v in range(VARS):
        for y in ORDER[6:]:
            finish(y, v)
        out_stage = finals.at[v]
        out_stage[...] = jnp.swapaxes(local[:, LEVB * v:LEVB * v + LEVB, :], 0, 1)
        outs.append(pltpu.make_async_copy(out_stage, out_ref.at[:, v], out_sem.at[v]))
        outs[-1].start()
    for copy in outs:
        copy.wait()
    for copy in sent:
        copy.wait_send()


def shards(
    increment, courant_x, courant_y, level_inverse, coupling, profile, send_column, send_block, send_count, obs_weight,
):
    vmem = pl.BlockSpec(memory_space=pltpu.VMEM)
    smem = pl.BlockSpec(memory_space=pltpu.SMEM)
    dma = pltpu.SemaphoreType.DMA
    return pl.pallas_call(
        kernel,
        out_shape=jax.ShapeDtypeStruct(increment.shape, F32),
        in_specs=[vmem] * 8 + [smem] * 2,
        out_specs=pl.BlockSpec(memory_space=pl.ANY),
        scratch_shapes=[
            pltpu.VMEM((4, ROWS + 2, LV, NX), F32),
            pltpu.VMEM((ROWS + 2, LEVB, NX), F32),
            pltpu.VMEM((5, ROWS, LEVB, NX), F32),
            pltpu.VMEM((4, ROWS, LEVB, NX), F32),
            pltpu.VMEM((ROWS, LV, NX), F32),
            pltpu.VMEM((2, 3 * LV, NX), BF16),
            pltpu.VMEM((2, LV + 16, 3 * LV), BF16),
            pltpu.VMEM((2, 128, 128), F32),
            pltpu.VMEM((2, 2, LV, 128), F32),
            pltpu.VMEM((LV, NBLK), F32),
            pltpu.VMEM((4, 2, VARS * ROWS, NX), F32),
            pltpu.VMEM((4, 3, VARS * ROWS, NX), F32),
            pltpu.VMEM((4, 3, 8, 128), F32),
            pltpu.VMEM((64, 1, 128), F32),
            pltpu.VMEM((64, 128), F32),
            pltpu.VMEM((128, 128), F32),
            pltpu.VMEM((128, 128), jnp.int32),
            pltpu.VMEM((CHUNKS, 1, CHUNK), jnp.int32),
            pltpu.VMEM((CHUNKS, 1, CHUNK), F32),
            pltpu.VMEM((8, 128), jnp.int32),
            pltpu.VMEM((CHUNKS, LV, CHUNK), F32),
            pltpu.VMEM((WINDOWS, 2 * LV, WIDE), BF16),
            pltpu.VMEM((PAIRS, WIDE, CHUNK), BF16),
            pltpu.VMEM((PAIRS, 1, CHUNK), F32),
            pltpu.VMEM((3, PAIRS, 1, CHUNK), F32),
            pltpu.VMEM((PAIRS, LV, WIDE), F32),
            pltpu.VMEM((VARS, LEVB, ROWS, NX), F32),
            pltpu.SMEM((8, 128), jnp.int32),
            dma((4, 2)), dma((4, 2)), dma((2,)), dma((2,)), dma((3,)), dma((3,)),
            dma((4, 3, 2)), dma((4, 3, 2)), dma((3,)), dma((3,)), dma((TILES - 1,)), dma((TILES - 1,)),
            dma, dma((VARS,)),
        ],
        compiler_params=pltpu.CompilerParams(
            collective_id=0, has_side_effects=True, vmem_limit_bytes=56 * 1024 * 1024),
    )(
        increment, courant_x, courant_y, level_inverse, profile,
        send_column.reshape(64, 128), send_block.reshape(64, 128), obs_weight.reshape(64, 1, 128),
        coupling, send_count,
    )


def solution(mesh):
    return jax.shard_map(
        shards,
        mesh=mesh,
        in_specs=(
            P("band", None, "tile", None),
            P("band", "tile", None),
            P("band", "tile", None),
            P(None, "band", None),
            P(),
            P("band", None, None),
            P("tile", None),
            P("tile", None),
            P("tile", None),
            P("tile", None),
        ),
        out_specs=P("band", None, "tile", None),
        check_vma=False,
    )
```

time: 122 us -> 77.7 us (0.64)
  Pallas kernels: 88.9 us -> 73.1 us
  other arithmetic: 14.8 us -> 0 us
  starting transfers between devices: 7.53 us -> 0 us
  local copies, waits for them, and re-layouts: 10.3 us -> 4.37 us
    pallas_call x1, Pallas kernels: 88.9 us -> 73.1 us  [shards(): pl.pallas_call(kernel, out_shape=jax.ShapeDtypeStruct(increment.shape, F3...]
    all_to_all x1 -> x0, starting transfers between devices: 7.53 us -> none  [shards(): lax.all_to_all(obs_weight.reshape(TILES, -1), 'tile', split_axis=0, conca...]
    sort x1 -> x0, other arithmetic: 6.92 us -> none  [shards(): key, weight = lax.sort((key, weight.reshape(-1)), num_keys=1)]
    slice x5 -> x0, local copies, waits for them, and re-layouts: 3.1 us -> none  [the longest x1 1.41 us: shards(): inverse[:, 0]]
    select_n x4 -> x0, other arithmetic: 2.03 us -> none  [the longest x1 0.69 us: shards(): base = jnp.where(valid, window * WIDE, -(1 << 20))]
    mul x4 -> x0, other arithmetic: 1.72 us -> none  [the longest x2 0.97 us: block_diagonal(): eye[:, None, :, None] * blocks[:, :, None, :]]
    lt x2 -> x0, other arithmetic: 1.42 us -> none  [the longest x1 0.73 us: shards(): weight = jnp.where(slot < send_count.reshape(TILES)[:, None], weight, 0.0)]
    another operation x5 -> x0, other arithmetic: 1.41 us -> none  [the longest x1 0.67 us: shards(): jnp.stack([first_column[:, 0], first_column[:, LEVB - 1], last_column[:,...]
  transfers between devices with their start and end apart: 1 -> 0, of which waited for: 0 -> 0; matrix products, arithmetic and copies ran while one was open for 8% -> 0% of each run, Pallas kernels for 0% -> 0%
where the time goes in v1:
time: 77.7 us; the launch traced here: 77.5 us
  Pallas kernels  73.1 us (94%)
  local copies, waits for them, and re-layouts  4.37 us (6%)
    pallas_call x1, Pallas kernels, shards(): pl.pallas_call(kernel, out_shape=jax.ShapeDtypeStruct(increment.shape, F3...  73.1 us
    unnamed x2, local copies, waits for them, and re-layouts  4.37 us

profile of v1, /device:TPU:0, one launch (start us, length us, event | category | flops | bytes accessed | tf_op | source)
XLA Modules:
  0.0 77.5 jit_solution(721846490383685268)
XLA Ops:
  0.0 1.4 %copy.11.prof_ref = f32[16,5,64]{2,1,0:T(8,128)} copy(f32[16,5,64]{2,0,1:T(8,128)} %param.15) | data formatting | bytes 40960 | tf_op args[5]
  1.4 73.1 %shard_map.100 = f32[16,5,8,768]{3,2,1,0:T(8,128)} custom-call(f32[16,5,8,768]{3,2,1,0:T(8,128)} %inc_ref.1, f32[16,8,768]{2,1,0:T(8,128)} %cx_ref.1, f32[16,8,768]{2,1,0:T(8,128)} %cy_ref.1, f32[5,16,16]{2,1,0:T(8,128)} %inv_ref.1, f32[16,5,64]{2,1,0:T(8,128)} %copy.11.prof_ref, s32[64,128]{1,0:T(8,128)} %bitcast.3, s32[64,128]{1,0:T(8,128)} %bitcast.4, ...), custom_call_target="tpu_custom_call" | custom-call | tf_op jit(solution)/shard_map/pallas_call | solution.py:480
  74.6 2.9 %copy.13 = f32[16,5,8,768]{3,2,1,0:T(8,128)} copy(f32[16,5,8,768]{3,2,1,0:T(8,128)} %shard_map.100) | data formatting | bytes 3932160

commit v2 on v1

--- a/solution.py
+++ b/solution.py
@@ -21,7 +21,8 @@
 WINDOWS = 24
 PAIRS = 56
 NBLK = 64
-ORDER = (1, 2, 3, 4, 5, 6, 0, 7)
+INNER_FIRST = (1, 2, 3, 4, 5, 6, 0, 7)
+OUTER_FIRST = (0, 7, 1, 2, 3, 4, 5, 6)
 SPLIT = 24
 F32 = jnp.float32
 BF16 = jnp.bfloat16
@@ -71,9 +72,9 @@
 def kernel(
     inc_ref, cx_ref, cy_ref, inv_ref, prof_ref, column_ref, block_ref, weight_ref, coupling_ref, count_ref,
     out_ref,
-    field, cyh, co, adj, local, stack, mext, gm, cols, tab, edges, recv, coefs, wbuf, wrow, turn, turn_key, keyr, wgtr, pairv,
+    field, cyh, co, adj, local, stack, mext, gm, cols, tab, edges, recv, beside, corner, coefs, wbuf, wrow, turn, turn_key, keyr, wgtr, pairv,
     ps, xs, onehot, val, valr, acc, finals, pair_ref,
-    halo_s, halo_r, cy_s, cy_r, cf_s, cf_r, ed_s, ed_r, va_s, va_r, wt_s, wt_r, pair_sem, out_sem,
+    first_s, first_r, halo_s, halo_r, diag_s, diag_r, cy_s, cy_r, cf_s, cf_r, ed_s, ed_r, va_s, va_r, wt_s, wt_r, pair_sem, out_sem,
 ):
     band = lax.axis_index("band")
     tile = lax.axis_index("tile")
@@ -87,7 +88,9 @@
             barrier, inc=1, device_id={"tile": lax.rem(tile + o, TILES)}, device_id_type=MESH)
     for p in partner:
         pl.semaphore_signal(barrier, inc=1, device_id={"band": p}, device_id_type=MESH)
-    pl.semaphore_wait(barrier, TILES + BANDS - 2)
+    for p in partner:
+        for t in (north, south):
+            pl.semaphore_signal(barrier, inc=1, device_id={"tile": t, "band": p}, device_id_type=MESH)
 
     sent = []
 
@@ -113,12 +116,11 @@
     for v in range(VARS):
         turned = jnp.swapaxes(inc_ref[:, v], 0, 1)
         field[0, 1:ROWS + 1, LEVB * v:LEVB * v + LEVB, :] = turned
-    halo1 = halo(field.at[0], halo_s.at[0], halo_r.at[0])
     gm[...] = jnp.zeros((2, 128, 128), F32)
     for v in range(VARS):
         rows = slice(LEVB * v, LEVB * v + LEVB)
         gm[0, rows, rows] = inv_ref[v]
-        tab[rows, :] = prof_ref[:, v, :]
+        tab[rows, :] = prof_ref[v]
     gm[1] = gm[0].T
     row_lane = lax.broadcasted_iota(jnp.int32, (8, 128), 1)
 
@@ -147,6 +149,8 @@
     coefs[0, 0] = across(firsts[0], scale_first)
     coefs[0, 1] = across(lasts[0], scale_first)
     coefs[0, 2] = across(firsts[0], scale_last)
+    pl.semaphore_wait(barrier, TILES + BANDS - 2 + 2 * (BANDS - 1))
+    halo1 = halo(field.at[0], first_s, first_r)
     cf_copies = [
         band_copy(coefs.at[0], coefs.at[o + 1], cf_s.at[o], cf_r.at[o], o) for o in range(3)
     ]
@@ -254,11 +258,11 @@
             + cs * field[src, y, rows, :] + cn * field[src, y + 2, rows, :]
         )
 
-    def solve(stage, kind, row_value, before_last, store_row, after_edges, gap=None):
-        copies = []
-        for k, y in enumerate(ORDER):
-            if k == 6:
-                before_last()
+    def solve(stage, kind, order, row_value, store_row, slot=None, before=None, gap=None):
+        copies, halos = [], []
+        for k, y in enumerate(order):
+            if k == 6 and before is not None:
+                before()
             for v in range(VARS):
                 high, low = halves(row_value(y, v))
                 rows = slice(LEVB * v, LEVB * v + LEVB)
@@ -266,9 +270,24 @@
                 stack[k % 2, LV + LEVB * v:LV + LEVB * v + LEVB, :] = low
                 stack[k % 2, 2 * LV + LEVB * v:2 * LV + LEVB * v + LEVB, :] = high
             result = mm(mext[kind], stack[k % 2])
-            local[y] = result[:LV]
+            local[stage, y] = result.reshape(12, 8, NX)
             edges[stage, 0, VARS * k:VARS * k + VARS, :] = result[LV:LV + VARS]
             edges[stage, 1, VARS * k:VARS * k + VARS, :] = result[LV + 8:LV + 8 + VARS]
+            if slot is not None and y in (0, ROWS - 1):
+                side, target = (1, south) if y == 0 else (0, north)
+                copy = pltpu.make_async_remote_copy(
+                    local.at[stage, y, 0:11], beside.at[slot, side], halo_s.at[slot, side], halo_r.at[slot, side],
+                    device_id={"tile": target}, device_id_type=MESH)
+                copy.start()
+                halos.append(copy)
+                for o in range(3):
+                    above = (band + o + 1) // BANDS
+                    copy = pltpu.make_async_remote_copy(
+                        local.at[stage, y, 10 + above], corner.at[slot, side, o],
+                        diag_s.at[slot, side, o], diag_r.at[slot, side, o],
+                        device_id={"tile": target, "band": partner[o]}, device_id_type=MESH)
+                    copy.start()
+                    halos.append(copy)
             for part, (at, lo, hi) in enumerate(((4, 0, SPLIT), (7, SPLIT, VARS * ROWS))):
                 if k == at:
                     for o in range(3):
@@ -276,28 +295,36 @@
                         copies.append(band_copy(
                             edges.at[stage, above, lo:hi], recv.at[stage, o, lo:hi],
                             ed_s.at[stage, o, part], ed_r.at[stage, o, part], o))
+        sent.extend(halos)
         if gap is not None:
             gap()
-        for copy in copies:
-            copy.wait_recv()
         _, own, low_c, high_c = chains[kind]
-        for y in (0, 7, 1, 2, 3, 4, 5, 6):
-            k = ORDER.index(y)
-            span = slice(VARS * k, VARS * k + VARS)
+
+        def complete(y, mine, got, parts):
             t = jnp.zeros((VARS, NX), F32)
-            s = wide(own[:VARS]) * edges[stage, 0, span, :]
+            s = wide(own[:VARS]) * mine
             for o in range(3):
-                got = recv[stage, o, span, :]
-                t = t + wide(low_c[o][:VARS]) * got
-                s = s + wide(high_c[o][:VARS]) * got
+                t = t + wide(low_c[o][:VARS]) * got[o]
+                s = s + wide(high_c[o][:VARS]) * got[o]
             for v in range(VARS):
                 rows = slice(LEVB * v, LEVB * v + LEVB)
                 left, right = wide(cols[kind, 0, rows, :]), wide(cols[kind, 1, rows, :])
-                store_row(y, v, local[y, rows, :] + left * t[v:v + 1] + right * s[v:v + 1])
-            if y == 7:
-                after_edges()
-
-    pending = {}
+                store_row(y, v, parts(v) + left * t[v:v + 1] + right * s[v:v + 1])
+
+        for copy in copies:
+            copy.wait_recv()
+        for k, y in enumerate(order):
+            span = slice(VARS * k, VARS * k + VARS)
+            complete(
+                y, edges[stage, 0, span, :], [recv[stage, o, span, :] for o in range(3)],
+                lambda v: local[stage, y, 2 * v:2 * v + 2].reshape(LEVB, NX))
+        for copy in halos:
+            copy.wait_recv()
+        if slot is not None:
+            for side, y in ((0, -1), (1, ROWS)):
+                complete(
+                    y, beside[slot, side, 10][:VARS], [corner[slot, side, o][:VARS] for o in range(3)],
+                    lambda v: beside[slot, side, 2 * v:2 * v + 2].reshape(LEVB, NX))
 
     def wait_halo(copies):
         for copy in copies:
@@ -307,11 +334,6 @@
         def store(y, v, value):
             field[index, y + 1, LEVB * v:LEVB * v + LEVB, :] = value
         return store
-
-    def send_field(index):
-        def send():
-            pending[index] = halo(field.at[index], halo_s.at[index], halo_r.at[index])
-        return send
 
     def store_state(y, v, value):
         high, low = halves(value)
@@ -395,8 +417,10 @@
 
         lax.fori_loop(0, PAIRS // 4, pick_cells, 0)
 
-    solve(0, 0, lambda y, v: stencil(0, y, v, 0), lambda: wait_halo(halo1), into_field(1), send_field(1), sort_slots)
-    solve(1, 0, lambda y, v: stencil(1, y, v, 0), lambda: wait_halo(pending[1]), store_state, lambda: None, pick_slots)
+    solve(
+        0, 0, INNER_FIRST, lambda y, v: stencil(0, y, v, 0), into_field(1), 0,
+        before=lambda: wait_halo(halo1), gap=sort_slots)
+    solve(1, 0, OUTER_FIRST, lambda y, v: stencil(1, y, v, 0), store_state, gap=pick_slots)
 
     def observe(i, carry):
         for u in range(4):
@@ -446,23 +470,15 @@
             parts.append(acc[pair_ref[4, w], LEVB * v:LEVB * v + LEVB, :] * some)
         return jnp.concatenate(parts, axis=1)
 
-    solve(2, 1, gradient, lambda: None, into_field(2), send_field(2))
-    solve(3, 1, lambda y, v: stencil(2, y, v, 1), lambda: wait_halo(pending[2]), into_field(3), send_field(3))
-
-    def finish(y, v):
-        rows = slice(LEVB * v, LEVB * v + LEVB)
-        local[y, rows, :] = stencil(3, y, v, 1) + field[0, y + 1, rows, :]
-
-    for y in ORDER[:6]:
-        for v in range(VARS):
-            finish(y, v)
-    wait_halo(pending[3])
+    solve(2, 1, OUTER_FIRST, gradient, into_field(2), 1)
+    solve(3, 1, OUTER_FIRST, lambda y, v: stencil(2, y, v, 1), into_field(3), 2)
+
     outs = []
     for v in range(VARS):
-        for y in ORDER[6:]:
-            finish(y, v)
+        rows = slice(LEVB * v, LEVB * v + LEVB)
+        result = [stencil(3, y, v, 1) + field[0, y + 1, rows, :] for y in range(ROWS)]
         out_stage = finals.at[v]
-        out_stage[...] = jnp.swapaxes(local[:, LEVB * v:LEVB * v + LEVB, :], 0, 1)
+        out_stage[...] = jnp.swapaxes(jnp.stack(result), 0, 1)
         outs.append(pltpu.make_async_copy(out_stage, out_ref.at[:, v], out_sem.at[v]))
         outs[-1].start()
     for copy in outs:
@@ -487,7 +503,7 @@
             pltpu.VMEM((ROWS + 2, LEVB, NX), F32),
             pltpu.VMEM((5, ROWS, LEVB, NX), F32),
             pltpu.VMEM((4, ROWS, LEVB, NX), F32),
-            pltpu.VMEM((ROWS, LV, NX), F32),
+            pltpu.VMEM((4, ROWS, 12, 8, NX), F32),
             pltpu.VMEM((2, 3 * LV, NX), BF16),
             pltpu.VMEM((2, LV + 16, 3 * LV), BF16),
             pltpu.VMEM((2, 128, 128), F32),
@@ -495,6 +511,8 @@
             pltpu.VMEM((LV, NBLK), F32),
             pltpu.VMEM((4, 2, VARS * ROWS, NX), F32),
             pltpu.VMEM((4, 3, VARS * ROWS, NX), F32),
+            pltpu.VMEM((3, 2, 11, 8, NX), F32),
+            pltpu.VMEM((3, 2, 3, 8, NX), F32),
             pltpu.VMEM((4, 3, 8, 128), F32),
             pltpu.VMEM((64, 1, 128), F32),
             pltpu.VMEM((64, 128), F32),
@@ -511,14 +529,15 @@
             pltpu.VMEM((PAIRS, LV, WIDE), F32),
             pltpu.VMEM((VARS, LEVB, ROWS, NX), F32),
             pltpu.SMEM((8, 128), jnp.int32),
-            dma((4, 2)), dma((4, 2)), dma((2,)), dma((2,)), dma((3,)), dma((3,)),
+            dma((2,)), dma((2,)), dma((3, 2)), dma((3, 2)), dma((3, 2, 3)), dma((3, 2, 3)),
+            dma((2,)), dma((2,)), dma((3,)), dma((3,)),
             dma((4, 3, 2)), dma((4, 3, 2)), dma((3,)), dma((3,)), dma((TILES - 1,)), dma((TILES - 1,)),
             dma, dma((VARS,)),
         ],
         compiler_params=pltpu.CompilerParams(
             collective_id=0, has_side_effects=True, vmem_limit_bytes=56 * 1024 * 1024),
     )(
-        increment, courant_x, courant_y, level_inverse, profile,
+        increment, courant_x, courant_y, level_inverse, profile.transpose(1, 0, 2),
         send_column.reshape(64, 128), send_block.reshape(64, 128), obs_weight.reshape(64, 1, 128),
         coupling, send_count,
     )

time: 77.7 us -> 72.6 us (0.934); the launches traced: 77.5 us -> 71.6 us
  Pallas kernels: 73.1 us -> 68.7 us
  local copies, waits for them, and re-layouts: 4.37 us -> 2.94 us
    pallas_call x1, Pallas kernels: 73.1 us -> 68.7 us  [shards(): pl.pallas_call(kernel, out_shape=jax.ShapeDtypeStruct(increment.shape, F3...]
    unnamed x2 -> x1, local copies, waits for them, and re-layouts: 4.37 us -> 2.94 us
where the time goes in v2:
time: 72.6 us; the launch traced here: 71.6 us
  Pallas kernels  68.7 us (95%)
  local copies, waits for them, and re-layouts  2.94 us (4%)
    pallas_call x1, Pallas kernels, shards(): pl.pallas_call(kernel, out_shape=jax.ShapeDtypeStruct(increment.shape, F3...  68.7 us
    unnamed x1, local copies, waits for them, and re-layouts  2.94 us

profile of v2, /device:TPU:0, one launch (start us, length us, event | category | flops | bytes accessed | tf_op | source)
XLA Modules:
  0.0 71.6 jit_solution(4187336714081695737)
XLA Ops:
  0.0 68.7 %shard_map.100 = f32[16,5,8,768]{3,2,1,0:T(8,128)} custom-call(f32[16,5,8,768]{3,2,1,0:T(8,128)} %inc_ref.1, f32[16,8,768]{2,1,0:T(8,128)} %cx_ref.1, f32[16,8,768]{2,1,0:T(8,128)} %cy_ref.1, f32[5,16,16]{2,1,0:T(8,128)} %inv_ref.1, f32[5,16,64]{2,1,0:T(8,128)} %bitcast.4, s32[64,128]{1,0:T(8,128)} %bitcast.5, s32[64,128]{1,0:T(8,128)} %bitcast.6, ...), custom_call_target="tpu_custom_call" | custom-call | tf_op jit(solution)/shard_map/pallas_call | solution.py:496
  68.7 2.9 %copy.12 = f32[16,5,8,768]{3,2,1,0:T(8,128)} copy(f32[16,5,8,768]{3,2,1,0:T(8,128)} %shard_map.100) | data formatting | bytes 3932160

commit v3 on v2

--- a/solution.py
+++ b/solution.py
@@ -22,6 +22,7 @@
 PAIRS = 56
 NBLK = 64
 INNER_FIRST = (1, 2, 3, 4, 5, 6, 0, 7)
+PARTS = ((0, 4), (4, 8), (8, 11), (11, 14))
 OUTER_FIRST = (0, 7, 1, 2, 3, 4, 5, 6)
 SPLIT = 24
 F32 = jnp.float32
@@ -72,9 +73,9 @@
 def kernel(
     inc_ref, cx_ref, cy_ref, inv_ref, prof_ref, column_ref, block_ref, weight_ref, coupling_ref, count_ref,
     out_ref,
-    field, cyh, co, adj, local, stack, mext, gm, cols, tab, edges, recv, beside, corner, coefs, wbuf, wrow, turn, turn_key, keyr, wgtr, pairv,
+    field, cyh, co, adj, local, stack, mext, gm, cols, tab, tabl, tabr, edges, recv, beside, corner, coefs, wbuf, wrow, turn, turn_key, keyr, wgtr, pairv,
     ps, xs, onehot, val, valr, acc, finals, pair_ref,
-    first_s, first_r, halo_s, halo_r, diag_s, diag_r, cy_s, cy_r, cf_s, cf_r, ed_s, ed_r, va_s, va_r, wt_s, wt_r, pair_sem, out_sem,
+    first_s, first_r, second_s, second_r, halo_s, halo_r, diag_s, diag_r, cy_s, cy_r, cf_s, cf_r, ed_s, ed_r, va_s, va_r, wt_s, wt_r, tab_s, tab_r, pair_sem, out_sem,
 ):
     band = lax.axis_index("band")
     tile = lax.axis_index("tile")
@@ -117,10 +118,11 @@
         turned = jnp.swapaxes(inc_ref[:, v], 0, 1)
         field[0, 1:ROWS + 1, LEVB * v:LEVB * v + LEVB, :] = turned
     gm[...] = jnp.zeros((2, 128, 128), F32)
+    tab[...] = jnp.zeros((LV, 128), F32)
     for v in range(VARS):
         rows = slice(LEVB * v, LEVB * v + LEVB)
         gm[0, rows, rows] = inv_ref[v]
-        tab[rows, :] = prof_ref[v]
+        tab[rows, 0:NBLK] = prof_ref[v]
     gm[1] = gm[0].T
     row_lane = lax.broadcasted_iota(jnp.int32, (8, 128), 1)
 
@@ -245,6 +247,12 @@
         high, low = halves(matrix)
         mext[kind] = jnp.concatenate([high, high, low], axis=1)
 
+    high, low = halves(tab[...])
+    tabl[...] = mm(mext[1], jnp.concatenate([high, low, high], axis=0)).reshape(12, 8, 128)
+    tab_copies = [
+        band_copy(tabl.at[10 + (band + o + 1) // BANDS], tabr.at[o], tab_s.at[o], tab_r.at[o], o) for o in range(3)
+    ]
+
     def stencil(src, y, v, kind):
         rows = slice(LEVB * v, LEVB * v + LEVB)
         f = field[src, y + 1, rows, :]
@@ -258,7 +266,7 @@
             + cs * field[src, y, rows, :] + cn * field[src, y + 2, rows, :]
         )
 
-    def solve(stage, kind, order, row_value, store_row, slot=None, before=None, gap=None):
+    def solve(stage, kind, order, row_value, store_row, before=None, gap=None):
         copies, halos = [], []
         for k, y in enumerate(order):
             if k == 6 and before is not None:
@@ -273,18 +281,18 @@
             local[stage, y] = result.reshape(12, 8, NX)
             edges[stage, 0, VARS * k:VARS * k + VARS, :] = result[LV:LV + VARS]
             edges[stage, 1, VARS * k:VARS * k + VARS, :] = result[LV + 8:LV + 8 + VARS]
-            if slot is not None and y in (0, ROWS - 1):
+            if y in (0, ROWS - 1):
                 side, target = (1, south) if y == 0 else (0, north)
                 copy = pltpu.make_async_remote_copy(
-                    local.at[stage, y, 0:11], beside.at[slot, side], halo_s.at[slot, side], halo_r.at[slot, side],
+                    local.at[stage, y, 0:11], beside.at[stage, side], halo_s.at[stage, side], halo_r.at[stage, side],
                     device_id={"tile": target}, device_id_type=MESH)
                 copy.start()
                 halos.append(copy)
                 for o in range(3):
                     above = (band + o + 1) // BANDS
                     copy = pltpu.make_async_remote_copy(
-                        local.at[stage, y, 10 + above], corner.at[slot, side, o],
-                        diag_s.at[slot, side, o], diag_r.at[slot, side, o],
+                        local.at[stage, y, 10 + above], corner.at[stage, side, o],
+                        diag_s.at[stage, side, o], diag_r.at[stage, side, o],
                         device_id={"tile": target, "band": partner[o]}, device_id_type=MESH)
                     copy.start()
                     halos.append(copy)
@@ -320,11 +328,10 @@
                 lambda v: local[stage, y, 2 * v:2 * v + 2].reshape(LEVB, NX))
         for copy in halos:
             copy.wait_recv()
-        if slot is not None:
-            for side, y in ((0, -1), (1, ROWS)):
-                complete(
-                    y, beside[slot, side, 10][:VARS], [corner[slot, side, o][:VARS] for o in range(3)],
-                    lambda v: beside[slot, side, 2 * v:2 * v + 2].reshape(LEVB, NX))
+        for side, y in ((0, -1), (1, ROWS)):
+            complete(
+                y, beside[stage, side, 10][:VARS], [corner[stage, side, o][:VARS] for o in range(3)],
+                lambda v: beside[stage, side, 2 * v:2 * v + 2].reshape(LEVB, NX))
 
     def wait_halo(copies):
         for copy in copies:
@@ -396,7 +403,20 @@
         copy.wait()
 
     def pick_slots():
-        profiles = jnp.concatenate(halves(tab[...]), axis=0)
+        for copy in tab_copies:
+            copy.wait_recv()
+        _, own, low_c, high_c = chains[1]
+        t = jnp.zeros((8, 128), F32)
+        s = own * tabl[10]
+        for o in range(3):
+            t = t + low_c[o] * tabr[o]
+            s = s + high_c[o] * tabr[o]
+        for v in range(VARS):
+            rows = slice(LEVB * v, LEVB * v + LEVB)
+            tab[rows, :] = (
+                tabl[2 * v:2 * v + 2].reshape(LEVB, 128)
+                + cols[1, 0, rows, :] * t[v:v + 1] + cols[1, 1, rows, :] * s[v:v + 1])
+        profiles = jnp.concatenate(halves(tab[:, 0:NBLK]), axis=0)
         block_iota = lax.broadcasted_iota(jnp.int32, (NBLK, CHUNK), 0)
         cell_iota = lax.broadcasted_iota(jnp.int32, (WIDE, CHUNK), 0)
 
@@ -417,10 +437,16 @@
 
         lax.fori_loop(0, PAIRS // 4, pick_cells, 0)
 
+    def gap():
+        sort_slots()
+        pick_slots()
+
     solve(
-        0, 0, INNER_FIRST, lambda y, v: stencil(0, y, v, 0), into_field(1), 0,
-        before=lambda: wait_halo(halo1), gap=sort_slots)
-    solve(1, 0, OUTER_FIRST, lambda y, v: stencil(1, y, v, 0), store_state, gap=pick_slots)
+        0, 0, INNER_FIRST, lambda y, v: stencil(0, y, v, 0), into_field(1),
+        before=lambda: wait_halo(halo1), gap=gap)
+    for y in range(ROWS):
+        for v in range(VARS):
+            store_state(y, v, stencil(1, y, v, 0))
 
     def observe(i, carry):
         for u in range(4):
@@ -430,8 +456,12 @@
             val[p] = jnp.sum(product, axis=0, keepdims=True)
         return carry
 
-    lax.fori_loop(0, PAIRS // 4, observe, 0)
-    copies = [band_copy(val, valr.at[o], va_s.at[o], va_r.at[o], o) for o in range(3)]
+    copies = []
+    for n, (begin, end) in enumerate(PARTS):
+        lax.fori_loop(begin, end, observe, 0)
+        span = slice(4 * begin, 4 * end)
+        copies.append([
+            band_copy(val.at[span], valr.at[o, span], va_s.at[n, o], va_r.at[n, o], o) for o in range(3)])
 
     wait_halo(halo_cy)
     for y in range(ROWS):
@@ -444,9 +474,6 @@
             ay = jnp.where(tile == TILES - 1, 0.0, ay)
         adj[2, y] = by
         adj[3, y] = ay
-    for copy in copies:
-        copy.wait_recv()
-
     def spread(i, before):
         for u in range(4):
             p = 4 * i + u
@@ -460,18 +487,20 @@
             acc[p] = before
         return before
 
-    lax.fori_loop(0, PAIRS // 4, spread, jnp.zeros((LV, WIDE), F32))
-
-    def gradient(y, v):
-        parts = []
+    total = jnp.zeros((LV, WIDE), F32)
+    for part, (begin, end) in zip(copies, PARTS):
+        wait_halo(part)
+        total = lax.fori_loop(begin, end, spread, total)
+
+    for y in OUTER_FIRST:
         for j in range(3):
             w = 3 * y + j
-            some = pair_ref[5, w].astype(F32)
-            parts.append(acc[pair_ref[4, w], LEVB * v:LEVB * v + LEVB, :] * some)
-        return jnp.concatenate(parts, axis=1)
-
-    solve(2, 1, OUTER_FIRST, gradient, into_field(2), 1)
-    solve(3, 1, OUTER_FIRST, lambda y, v: stencil(2, y, v, 1), into_field(3), 2)
+            field[2, y + 1, :, WIDE * j:WIDE * j + WIDE] = acc[pair_ref[4, w]] * pair_ref[5, w].astype(F32)
+        if y == ROWS - 1:
+            halo2 = halo(field.at[2], second_s, second_r)
+    solve(
+        1, 1, INNER_FIRST, lambda y, v: stencil(2, y, v, 1), into_field(3),
+        before=lambda: wait_halo(halo2))
 
     outs = []
     for v in range(VARS):
@@ -503,16 +532,18 @@
             pltpu.VMEM((ROWS + 2, LEVB, NX), F32),
             pltpu.VMEM((5, ROWS, LEVB, NX), F32),
             pltpu.VMEM((4, ROWS, LEVB, NX), F32),
-            pltpu.VMEM((4, ROWS, 12, 8, NX), F32),
+            pltpu.VMEM((2, ROWS, 12, 8, NX), F32),
             pltpu.VMEM((2, 3 * LV, NX), BF16),
             pltpu.VMEM((2, LV + 16, 3 * LV), BF16),
             pltpu.VMEM((2, 128, 128), F32),
             pltpu.VMEM((2, 2, LV, 128), F32),
-            pltpu.VMEM((LV, NBLK), F32),
-            pltpu.VMEM((4, 2, VARS * ROWS, NX), F32),
-            pltpu.VMEM((4, 3, VARS * ROWS, NX), F32),
-            pltpu.VMEM((3, 2, 11, 8, NX), F32),
-            pltpu.VMEM((3, 2, 3, 8, NX), F32),
+            pltpu.VMEM((LV, 128), F32),
+            pltpu.VMEM((12, 8, 128), F32),
+            pltpu.VMEM((3, 8, 128), F32),
+            pltpu.VMEM((2, 2, VARS * ROWS, NX), F32),
+            pltpu.VMEM((2, 3, VARS * ROWS, NX), F32),
+            pltpu.VMEM((2, 2, 11, 8, NX), F32),
+            pltpu.VMEM((2, 2, 3, 8, NX), F32),
             pltpu.VMEM((4, 3, 8, 128), F32),
             pltpu.VMEM((64, 1, 128), F32),
             pltpu.VMEM((64, 128), F32),
@@ -529,9 +560,10 @@
             pltpu.VMEM((PAIRS, LV, WIDE), F32),
             pltpu.VMEM((VARS, LEVB, ROWS, NX), F32),
             pltpu.SMEM((8, 128), jnp.int32),
-            dma((2,)), dma((2,)), dma((3, 2)), dma((3, 2)), dma((3, 2, 3)), dma((3, 2, 3)),
+            dma((2,)), dma((2,)), dma((2,)), dma((2,)), dma((2, 2)), dma((2, 2)), dma((2, 2, 3)), dma((2, 2, 3)),
             dma((2,)), dma((2,)), dma((3,)), dma((3,)),
-            dma((4, 3, 2)), dma((4, 3, 2)), dma((3,)), dma((3,)), dma((TILES - 1,)), dma((TILES - 1,)),
+            dma((2, 3, 2)), dma((2, 3, 2)), dma((4, 3)), dma((4, 3)), dma((TILES - 1,)), dma((TILES - 1,)),
+            dma((3,)), dma((3,)),
             dma, dma((VARS,)),
         ],
         compiler_params=pltpu.CompilerParams(

time: 72.6 us -> 59.7 us (0.82); the launches traced: 71.6 us -> 59.5 us
  Pallas kernels: 68.7 us -> 56.6 us
    pallas_call x1, Pallas kernels: 68.7 us -> 56.6 us  [shards(): pl.pallas_call(kernel, out_shape=jax.ShapeDtypeStruct(increment.shape, F3...]
where the time goes in v3:
time: 59.7 us; the launch traced here: 59.5 us
  Pallas kernels  56.6 us (95%)
  local copies, waits for them, and re-layouts  2.94 us (5%)
    pallas_call x1, Pallas kernels, shards(): pl.pallas_call(kernel, out_shape=jax.ShapeDtypeStruct(increment.shape, F3...  56.6 us
    unnamed x1, local copies, waits for them, and re-layouts  2.94 us

profile of v3, /device:TPU:0, one launch (start us, length us, event | category | flops | bytes accessed | tf_op | source)
XLA Modules:
  0.0 59.5 jit_solution(2122144242093022588)
XLA Ops:
  0.0 56.6 %shard_map.100 = f32[16,5,8,768]{3,2,1,0:T(8,128)} custom-call(f32[16,5,8,768]{3,2,1,0:T(8,128)} %inc_ref.1, f32[16,8,768]{2,1,0:T(8,128)} %cx_ref.1, f32[16,8,768]{2,1,0:T(8,128)} %cy_ref.1, f32[5,16,16]{2,1,0:T(8,128)} %inv_ref.1, f32[5,16,64]{2,1,0:T(8,128)} %bitcast.4, s32[64,128]{1,0:T(8,128)} %bitcast.5, s32[64,128]{1,0:T(8,128)} %bitcast.6, ...), custom_call_target="tpu_custom_call" | custom-call | tf_op jit(solution)/shard_map/pallas_call | solution.py:525
  56.6 2.9 %copy.12 = f32[16,5,8,768]{3,2,1,0:T(8,128)} copy(f32[16,5,8,768]{3,2,1,0:T(8,128)} %shard_map.100) | data formatting | bytes 3932160

commit v4 on v3

--- a/solution.py
+++ b/solution.py
@@ -23,7 +23,6 @@
 NBLK = 64
 INNER_FIRST = (1, 2, 3, 4, 5, 6, 0, 7)
 PARTS = ((0, 4), (4, 8), (8, 11), (11, 14))
-OUTER_FIRST = (0, 7, 1, 2, 3, 4, 5, 6)
 SPLIT = 24
 F32 = jnp.float32
 BF16 = jnp.bfloat16
@@ -71,11 +70,11 @@
 
 
 def kernel(
-    inc_ref, cx_ref, cy_ref, inv_ref, prof_ref, column_ref, block_ref, weight_ref, coupling_ref, count_ref,
+    inc_hbm, cx_hbm, cy_hbm, inv_ref, prof_ref, column_ref, block_ref, weight_ref, coupling_ref, count_ref,
     out_ref,
-    field, cyh, co, adj, local, stack, mext, gm, cols, tab, tabl, tabr, edges, recv, beside, corner, coefs, wbuf, wrow, turn, turn_key, keyr, wgtr, pairv,
-    ps, xs, onehot, val, valr, acc, finals, pair_ref,
-    first_s, first_r, second_s, second_r, halo_s, halo_r, diag_s, diag_r, cy_s, cy_r, cf_s, cf_r, ed_s, ed_r, va_s, va_r, wt_s, wt_r, tab_s, tab_r, pair_sem, out_sem,
+    field, cyh, co, adj, partial, local, stack, mext, gm, cols, tab, tabl, tabr, edges, recv, beside, corner, coefs, wbuf, wrow, turn, turn_key, keyr, wgtr, pairv,
+    ps, xs, onehot, val, valr, acc, inc_ref, cx_ref, cy_ref, pair_ref,
+    first_s, first_r, second_s, second_r, halo_s, halo_r, diag_s, diag_r, cy_s, cy_r, cf_s, cf_r, ed_s, ed_r, va_s, va_r, wt_s, wt_r, tab_s, tab_r, pair_sem, out_sem, in_sem,
 ):
     band = lax.axis_index("band")
     tile = lax.axis_index("tile")
@@ -107,6 +106,18 @@
         sent.extend([up, down])
         return up, down
 
+    def halo_part(buffer, c, send, receive):
+        cols = slice(WIDE * c, WIDE * c + WIDE)
+        pair = []
+        for n, (source, target, place) in enumerate(((ROWS, north, 0), (1, south, ROWS + 1))):
+            copy = pltpu.make_async_remote_copy(
+                buffer.at[source, :, cols], buffer.at[place, :, cols], send.at[n, c], receive.at[n, c],
+                device_id={"tile": target}, device_id_type=MESH)
+            copy.start()
+            pair.append(copy)
+        sent.extend(pair)
+        return pair
+
     def band_copy(source, target, send, receive, o):
         copy = pltpu.make_async_remote_copy(
             source, target, send, receive, device_id={"band": partner[o]}, device_id_type=MESH)
@@ -114,9 +125,12 @@
         sent.append(copy)
         return copy
 
-    for v in range(VARS):
-        turned = jnp.swapaxes(inc_ref[:, v], 0, 1)
-        field[0, 1:ROWS + 1, LEVB * v:LEVB * v + LEVB, :] = turned
+    loads = [pltpu.make_async_copy(inc_hbm.at[:, v], inc_ref.at[v], in_sem.at[v]) for v in range(VARS)]
+    loads.append(pltpu.make_async_copy(cy_hbm, cy_ref, in_sem.at[VARS]))
+    loads.append(pltpu.make_async_copy(cx_hbm, cx_ref, in_sem.at[VARS + 1]))
+    for copy in loads:
+        copy.start()
+
     gm[...] = jnp.zeros((2, 128, 128), F32)
     tab[...] = jnp.zeros((LV, 128), F32)
     for v in range(VARS):
@@ -148,11 +162,15 @@
     def across(value, weight):
         return jnp.broadcast_to(jnp.sum(value * weight[0:1], axis=1, keepdims=True), (value.shape[0], 128))
 
+    for v in range(VARS):
+        loads[v].wait()
+        turned = jnp.swapaxes(inc_ref[v], 0, 1)
+        field[0, 1:ROWS + 1, LEVB * v:LEVB * v + LEVB, :] = turned
     coefs[0, 0] = across(firsts[0], scale_first)
     coefs[0, 1] = across(lasts[0], scale_first)
     coefs[0, 2] = across(firsts[0], scale_last)
     pl.semaphore_wait(barrier, TILES + BANDS - 2 + 2 * (BANDS - 1))
-    halo1 = halo(field.at[0], first_s, first_r)
+    halo1 = [halo_part(field.at[0], c, first_s, first_r) for c in range(3)]
     cf_copies = [
         band_copy(coefs.at[0], coefs.at[o + 1], cf_s.at[o], cf_r.at[o], o) for o in range(3)
     ]
@@ -170,6 +188,8 @@
         copy.start()
         sent.append(copy)
         wt_copies.append(copy)
+    loads[VARS].wait()
+    loads[VARS + 1].wait()
     cyh[1:ROWS + 1] = jnp.swapaxes(cy_ref[...], 0, 1)
     halo_cy = halo(cyh, cy_s, cy_r)
     co[0] = jnp.swapaxes(cx_ref[...], 0, 1)
@@ -253,56 +273,74 @@
         band_copy(tabl.at[10 + (band + o + 1) // BANDS], tabr.at[o], tab_s.at[o], tab_r.at[o], o) for o in range(3)
     ]
 
-    def stencil(src, y, v, kind):
+    def stencil(src, y, v, kind, below=True, above=True):
         rows = slice(LEVB * v, LEVB * v + LEVB)
         f = field[src, y + 1, rows, :]
         west, east = pltpu.roll(f, 1, 1), pltpu.roll(f, NX - 1, 1)
-        if kind == 0:
-            cw, ce, cs, cn = (co[i, y] for i in (1, 2, 3, 4))
-        else:
-            cw, ce, cs, cn = adj[0, y], adj[1, y], adj[2, y], adj[3, y]
-        return (
-            co[0, y] * f + cw * west + ce * east
-            + cs * field[src, y, rows, :] + cn * field[src, y + 2, rows, :]
-        )
-
-    def solve(stage, kind, order, row_value, store_row, before=None, gap=None):
+        cw, ce = (co[1, y], co[2, y]) if kind == 0 else (adj[0, y], adj[1, y])
+        result = co[0, y] * f + cw * west + ce * east
+        if below:
+            result = result + (co[3, y] if kind == 0 else adj[2, y]) * field[src, y, rows, :]
+        if above:
+            result = result + (co[4, y] if kind == 0 else adj[3, y]) * field[src, y + 2, rows, :]
+        return result
+
+    def solve(stage, kind, src, arrivals, store_row, gap=None):
         copies, halos = [], []
-        for k, y in enumerate(order):
-            if k == 6 and before is not None:
-                before()
+        order = INNER_FIRST
+
+        def multiply(y, k, slot, part_cols, value):
             for v in range(VARS):
-                high, low = halves(row_value(y, v))
-                rows = slice(LEVB * v, LEVB * v + LEVB)
-                stack[k % 2, rows, :] = high
-                stack[k % 2, LV + LEVB * v:LV + LEVB * v + LEVB, :] = low
-                stack[k % 2, 2 * LV + LEVB * v:2 * LV + LEVB * v + LEVB, :] = high
-            result = mm(mext[kind], stack[k % 2])
-            local[stage, y] = result.reshape(12, 8, NX)
-            edges[stage, 0, VARS * k:VARS * k + VARS, :] = result[LV:LV + VARS]
-            edges[stage, 1, VARS * k:VARS * k + VARS, :] = result[LV + 8:LV + 8 + VARS]
-            if y in (0, ROWS - 1):
-                side, target = (1, south) if y == 0 else (0, north)
+                high, low = halves(value(v))
+                for n, half in enumerate((high, low, high)):
+                    stack[slot, LV * n + LEVB * v:LV * n + LEVB * v + LEVB, part_cols] = half
+            result = mm(mext[kind], stack[slot, :, part_cols])
+            local[stage, y, :, :, part_cols] = result.reshape(12, 8, result.shape[1])
+            edges[stage, 0, VARS * k:VARS * k + VARS, part_cols] = result[LV:LV + VARS]
+            edges[stage, 1, VARS * k:VARS * k + VARS, part_cols] = result[LV + 8:LV + 8 + VARS]
+
+        def send_edges(part, lo, hi):
+            for o in range(3):
+                above = (band + o + 1) // BANDS
+                copies.append(band_copy(
+                    edges.at[stage, above, lo:hi], recv.at[stage, o, lo:hi],
+                    ed_s.at[stage, o, part], ed_r.at[stage, o, part], o))
+
+        for k, y in enumerate(order[:6]):
+            multiply(y, k, k % 2, slice(0, NX), lambda v: stencil(src, y, v, kind))
+            if k == 4:
+                send_edges(0, 0, SPLIT)
+        outer = ((0, 0, 1, south), (ROWS - 1, ROWS + 1, 0, north))
+        for i, (y, beyond, side, target) in enumerate(outer):
+            for v in range(VARS):
+                partial[i, LEVB * v:LEVB * v + LEVB, :] = stencil(src, y, v, kind, y > 0, y == 0)
+        for c in range(3):
+            part_cols = slice(WIDE * c, WIDE * c + WIDE)
+            wait_halo(arrivals[c])
+            for i, (y, beyond, side, target) in enumerate(outer):
+                factor = (co[3 + i, y, :, part_cols]) if kind == 0 else adj[2 + i, y, :, part_cols]
+
+                def value(v):
+                    rows = slice(LEVB * v, LEVB * v + LEVB)
+                    return partial[i, rows, part_cols] + factor * field[src, beyond, rows, part_cols]
+
+                multiply(y, 6 + i, i, part_cols, value)
                 copy = pltpu.make_async_remote_copy(
-                    local.at[stage, y, 0:11], beside.at[stage, side], halo_s.at[stage, side], halo_r.at[stage, side],
+                    local.at[stage, y, 0:11, :, part_cols], beside.at[stage, side, :, :, part_cols],
+                    halo_s.at[stage, side, c], halo_r.at[stage, side, c],
                     device_id={"tile": target}, device_id_type=MESH)
                 copy.start()
                 halos.append(copy)
-                for o in range(3):
-                    above = (band + o + 1) // BANDS
-                    copy = pltpu.make_async_remote_copy(
-                        local.at[stage, y, 10 + above], corner.at[stage, side, o],
-                        diag_s.at[stage, side, o], diag_r.at[stage, side, o],
-                        device_id={"tile": target, "band": partner[o]}, device_id_type=MESH)
-                    copy.start()
-                    halos.append(copy)
-            for part, (at, lo, hi) in enumerate(((4, 0, SPLIT), (7, SPLIT, VARS * ROWS))):
-                if k == at:
-                    for o in range(3):
-                        above = (band + o + 1) // BANDS
-                        copies.append(band_copy(
-                            edges.at[stage, above, lo:hi], recv.at[stage, o, lo:hi],
-                            ed_s.at[stage, o, part], ed_r.at[stage, o, part], o))
+        send_edges(1, SPLIT, VARS * ROWS)
+        for y, beyond, side, target in outer:
+            for o in range(3):
+                above = (band + o + 1) // BANDS
+                copy = pltpu.make_async_remote_copy(
+                    local.at[stage, y, 10 + above], corner.at[stage, side, o],
+                    diag_s.at[stage, side, o], diag_r.at[stage, side, o],
+                    device_id={"tile": target, "band": partner[o]}, device_id_type=MESH)
+                copy.start()
+                halos.append(copy)
         sent.extend(halos)
         if gap is not None:
             gap()
@@ -441,9 +479,7 @@
         sort_slots()
         pick_slots()
 
-    solve(
-        0, 0, INNER_FIRST, lambda y, v: stencil(0, y, v, 0), into_field(1),
-        before=lambda: wait_halo(halo1), gap=gap)
+    solve(0, 0, 0, halo1, into_field(1), gap)
     for y in range(ROWS):
         for v in range(VARS):
             store_state(y, v, stencil(1, y, v, 0))
@@ -492,21 +528,25 @@
         wait_halo(part)
         total = lax.fori_loop(begin, end, spread, total)
 
-    for y in OUTER_FIRST:
+    def place_gradient(y, j):
+        w = 3 * y + j
+        field[2, y + 1, :, WIDE * j:WIDE * j + WIDE] = acc[pair_ref[4, w]] * pair_ref[5, w].astype(F32)
+
+    halo2 = []
+    for j in range(3):
+        for y in (0, ROWS - 1):
+            place_gradient(y, j)
+        halo2.append(halo_part(field.at[2], j, second_s, second_r))
+    for y in INNER_FIRST[:6]:
         for j in range(3):
-            w = 3 * y + j
-            field[2, y + 1, :, WIDE * j:WIDE * j + WIDE] = acc[pair_ref[4, w]] * pair_ref[5, w].astype(F32)
-        if y == ROWS - 1:
-            halo2 = halo(field.at[2], second_s, second_r)
-    solve(
-        1, 1, INNER_FIRST, lambda y, v: stencil(2, y, v, 1), into_field(3),
-        before=lambda: wait_halo(halo2))
+            place_gradient(y, j)
+    solve(1, 1, 2, halo2, into_field(3))
 
     outs = []
     for v in range(VARS):
         rows = slice(LEVB * v, LEVB * v + LEVB)
         result = [stencil(3, y, v, 1) + field[0, y + 1, rows, :] for y in range(ROWS)]
-        out_stage = finals.at[v]
+        out_stage = inc_ref.at[v]
         out_stage[...] = jnp.swapaxes(jnp.stack(result), 0, 1)
         outs.append(pltpu.make_async_copy(out_stage, out_ref.at[:, v], out_sem.at[v]))
         outs[-1].start()
@@ -520,18 +560,20 @@
     increment, courant_x, courant_y, level_inverse, coupling, profile, send_column, send_block, send_count, obs_weight,
 ):
     vmem = pl.BlockSpec(memory_space=pltpu.VMEM)
+    any_space = pl.BlockSpec(memory_space=pl.ANY)
     smem = pl.BlockSpec(memory_space=pltpu.SMEM)
     dma = pltpu.SemaphoreType.DMA
     return pl.pallas_call(
         kernel,
         out_shape=jax.ShapeDtypeStruct(increment.shape, F32),
-        in_specs=[vmem] * 8 + [smem] * 2,
-        out_specs=pl.BlockSpec(memory_space=pl.ANY),
+        in_specs=[any_space] * 3 + [vmem] * 5 + [smem] * 2,
+        out_specs=any_space,
         scratch_shapes=[
             pltpu.VMEM((4, ROWS + 2, LV, NX), F32),
             pltpu.VMEM((ROWS + 2, LEVB, NX), F32),
             pltpu.VMEM((5, ROWS, LEVB, NX), F32),
             pltpu.VMEM((4, ROWS, LEVB, NX), F32),
+            pltpu.VMEM((2, LV, NX), F32),
             pltpu.VMEM((2, ROWS, 12, 8, NX), F32),
             pltpu.VMEM((2, 3 * LV, NX), BF16),
             pltpu.VMEM((2, LV + 16, 3 * LV), BF16),
@@ -559,12 +601,14 @@
             pltpu.VMEM((3, PAIRS, 1, CHUNK), F32),
             pltpu.VMEM((PAIRS, LV, WIDE), F32),
             pltpu.VMEM((VARS, LEVB, ROWS, NX), F32),
+            pltpu.VMEM((LEVB, ROWS, NX), F32),
+            pltpu.VMEM((LEVB, ROWS, NX), F32),
             pltpu.SMEM((8, 128), jnp.int32),
-            dma((2,)), dma((2,)), dma((2,)), dma((2,)), dma((2, 2)), dma((2, 2)), dma((2, 2, 3)), dma((2, 2, 3)),
+            dma((2, 3)), dma((2, 3)), dma((2, 3)), dma((2, 3)), dma((2, 2, 3)), dma((2, 2, 3)), dma((2, 2, 3)), dma((2, 2, 3)),
             dma((2,)), dma((2,)), dma((3,)), dma((3,)),
             dma((2, 3, 2)), dma((2, 3, 2)), dma((4, 3)), dma((4, 3)), dma((TILES - 1,)), dma((TILES - 1,)),
             dma((3,)), dma((3,)),
-            dma, dma((VARS,)),
+            dma, dma((VARS,)), dma((VARS + 2,)),
         ],
         compiler_params=pltpu.CompilerParams(
             collective_id=0, has_side_effects=True, vmem_limit_bytes=56 * 1024 * 1024),

time: 59.7 us -> 56 us (0.938)
  Pallas kernels: 56.6 us -> 52.8 us
    pallas_call x1, Pallas kernels: 56.6 us -> 52.8 us  [shards(): pl.pallas_call(kernel, out_shape=jax.ShapeDtypeStruct(increment.shape, F3...]
where the time goes in v4:
time: 56 us; the launch traced here: 55.8 us
  Pallas kernels  52.8 us (94%)
  local copies, waits for them, and re-layouts  2.94 us (5%)
    pallas_call x1, Pallas kernels, shards(): pl.pallas_call(kernel, out_shape=jax.ShapeDtypeStruct(increment.shape, F3...  52.8 us
    unnamed x1, local copies, waits for them, and re-layouts  2.94 us

profile of v4, /device:TPU:0, one launch (start us, length us, event | category | flops | bytes accessed | tf_op | source)
XLA Modules:
  0.0 55.8 jit_solution(18008172332893673032)
XLA Ops:
  0.0 52.8 %shard_map.100 = f32[16,5,8,768]{3,2,1,0:T(8,128)} custom-call(f32[16,5,8,768]{3,2,1,0:T(8,128)} %inc_hbm.1, f32[16,8,768]{2,1,0:T(8,128)} %cx_hbm.1, f32[16,8,768]{2,1,0:T(8,128)} %cy_hbm.1, f32[5,16,16]{2,1,0:T(8,128)} %inv_ref.1, f32[5,16,64]{2,1,0:T(8,128)} %bitcast.4, s32[64,128]{1,0:T(8,128)} %bitcast.5, s32[64,128]{1,0:T(8,128)} %bitcast.6, ...), custom_call_target="tpu_custom_call" | custom-call | tf_op jit(solution)/shard_map/pallas_call | solution.py:566
  52.8 2.9 %copy.12 = f32[16,5,8,768]{3,2,1,0:T(8,128)} copy(f32[16,5,8,768]{3,2,1,0:T(8,128)} %shard_map.100) | data formatting | bytes 3932160

commit v5 on v4

--- a/solution.py
+++ b/solution.py
@@ -22,7 +22,7 @@
 PAIRS = 56
 NBLK = 64
 INNER_FIRST = (1, 2, 3, 4, 5, 6, 0, 7)
-PARTS = ((0, 4), (4, 8), (8, 11), (11, 14))
+PARTS = ((0, 2), (2, 4), (4, 6), (6, 7))
 SPLIT = 24
 F32 = jnp.float32
 BF16 = jnp.bfloat16
@@ -285,7 +285,7 @@
             result = result + (co[4, y] if kind == 0 else adj[3, y]) * field[src, y + 2, rows, :]
         return result
 
-    def solve(stage, kind, src, arrivals, store_row, gap=None):
+    def solve(stage, kind, src, arrivals, store_row, inner, gap=None):
         copies, halos = [], []
         order = INNER_FIRST
 
@@ -364,6 +364,7 @@
             complete(
                 y, edges[stage, 0, span, :], [recv[stage, o, span, :] for o in range(3)],
                 lambda v: local[stage, y, 2 * v:2 * v + 2].reshape(LEVB, NX))
+        inner()
         for copy in halos:
             copy.wait_recv()
         for side, y in ((0, -1), (1, ROWS)):
@@ -479,14 +480,17 @@
         sort_slots()
         pick_slots()
 
-    solve(0, 0, 0, halo1, into_field(1), gap)
-    for y in range(ROWS):
-        for v in range(VARS):
-            store_state(y, v, stencil(1, y, v, 0))
+    def observe_rows(rows):
+        for y in rows:
+            for v in range(VARS):
+                store_state(y, v, stencil(1, y, v, 0))
+
+    solve(0, 0, 0, halo1, into_field(1), lambda: observe_rows(INNER_FIRST[:6]), gap)
+    observe_rows(INNER_FIRST[6:])
 
     def observe(i, carry):
-        for u in range(4):
-            p = 4 * i + u
+        for u in range(8):
+            p = 8 * i + u
             picked = mm(xs[pair_ref[1, p]], onehot[p])
             product = (picked[:LV] + picked[LV:]) * ps[pair_ref[0, p]]
             val[p] = jnp.sum(product, axis=0, keepdims=True)
@@ -495,7 +499,7 @@
     copies = []
     for n, (begin, end) in enumerate(PARTS):
         lax.fori_loop(begin, end, observe, 0)
-        span = slice(4 * begin, 4 * end)
+        span = slice(8 * begin, 8 * end)
         copies.append([
             band_copy(val.at[span], valr.at[o, span], va_s.at[n, o], va_r.at[n, o], o) for o in range(3)])
 
@@ -511,8 +515,8 @@
         adj[2, y] = by
         adj[3, y] = ay
     def spread(i, before):
-        for u in range(4):
-            p = 4 * i + u
+        for u in range(8):
+            p = 8 * i + u
             c = pair_ref[0, p]
             values = (val[p] + valr[0, p]) + (valr[1, p] + valr[2, p])
             high, low = halves(ps[c] * (values * wgtr[c]))
@@ -540,14 +544,22 @@
     for y in INNER_FIRST[:6]:
         for j in range(3):
             place_gradient(y, j)
-    solve(1, 1, 2, halo2, into_field(3))
-
+    def finish(y, v):
+        rows = slice(LEVB * v, LEVB * v + LEVB)
+        field[1, y + 1, rows, :] = stencil(3, y, v, 1) + field[0, y + 1, rows, :]
+
+    def finish_inner():
+        for y in INNER_FIRST[:6]:
+            for v in range(VARS):
+                finish(y, v)
+
+    solve(1, 1, 2, halo2, into_field(3), finish_inner)
     outs = []
     for v in range(VARS):
-        rows = slice(LEVB * v, LEVB * v + LEVB)
-        result = [stencil(3, y, v, 1) + field[0, y + 1, rows, :] for y in range(ROWS)]
+        for y in INNER_FIRST[6:]:
+            finish(y, v)
         out_stage = inc_ref.at[v]
-        out_stage[...] = jnp.swapaxes(jnp.stack(result), 0, 1)
+        out_stage[...] = jnp.swapaxes(field[1, 1:ROWS + 1, LEVB * v:LEVB * v + LEVB, :], 0, 1)
         outs.append(pltpu.make_async_copy(out_stage, out_ref.at[:, v], out_sem.at[v]))
         outs[-1].start()
     for copy in outs:

time: 56 us -> 53.7 us (0.959)
  Pallas kernels: 52.8 us -> 50.5 us
    pallas_call x1, Pallas kernels: 52.8 us -> 50.5 us  [shards(): pl.pallas_call(kernel, out_shape=jax.ShapeDtypeStruct(increment.shape, F3...]
where the time goes in v5:
time: 53.7 us; the launch traced here: 53.4 us
  Pallas kernels  50.5 us (94%)
  local copies, waits for them, and re-layouts  2.94 us (5%)
    pallas_call x1, Pallas kernels, shards(): pl.pallas_call(kernel, out_shape=jax.ShapeDtypeStruct(increment.shape, F3...  50.5 us
    unnamed x1, local copies, waits for them, and re-layouts  2.94 us

profile of v5, /device:TPU:0, one launch (start us, length us, event | category | flops | bytes accessed | tf_op | source)
XLA Modules:
  0.0 53.4 jit_solution(2485052260901986330)
XLA Ops:
  0.0 50.5 %shard_map.100 = f32[16,5,8,768]{3,2,1,0:T(8,128)} custom-call(f32[16,5,8,768]{3,2,1,0:T(8,128)} %inc_hbm.1, f32[16,8,768]{2,1,0:T(8,128)} %cx_hbm.1, f32[16,8,768]{2,1,0:T(8,128)} %cy_hbm.1, f32[5,16,16]{2,1,0:T(8,128)} %inv_ref.1, f32[5,16,64]{2,1,0:T(8,128)} %bitcast.4, s32[64,128]{1,0:T(8,128)} %bitcast.5, s32[64,128]{1,0:T(8,128)} %bitcast.6, ...), custom_call_target="tpu_custom_call" | custom-call | tf_op jit(solution)/shard_map/pallas_call | solution.py:578
  50.5 2.9 %copy.12 = f32[16,5,8,768]{3,2,1,0:T(8,128)} copy(f32[16,5,8,768]{3,2,1,0:T(8,128)} %shard_map.100) | data formatting | bytes 3932160

commit v6 on v5

--- a/solution.py
+++ b/solution.py
@@ -22,7 +22,7 @@
 PAIRS = 56
 NBLK = 64
 INNER_FIRST = (1, 2, 3, 4, 5, 6, 0, 7)
-PARTS = ((0, 2), (2, 4), (4, 6), (6, 7))
+PARTS = ((0, 1), (1, 2), (2, 3), (3, 4))
 SPLIT = 24
 F32 = jnp.float32
 BF16 = jnp.bfloat16
@@ -460,21 +460,21 @@
         cell_iota = lax.broadcasted_iota(jnp.int32, (WIDE, CHUNK), 0)
 
         def pick_profiles(i, carry):
-            for u in range(4):
-                c = 4 * i + u
+            for u in range(8):
+                c = 8 * i + u
                 picked = mm(profiles, (block_iota == keyr[c] % NBLK).astype(BF16))
                 ps[c] = picked[:LV] + picked[LV:]
             return carry
 
-        lax.fori_loop(0, CHUNKS // 4, pick_profiles, 0)
+        lax.fori_loop(0, CHUNKS // 8, pick_profiles, 0)
 
         def pick_cells(i, carry):
-            for u in range(4):
-                p = 4 * i + u
+            for u in range(8):
+                p = 8 * i + u
                 onehot[p] = (cell_iota == keyr[pair_ref[0, p]] // NBLK - pair_ref[2, p]).astype(BF16)
             return carry
 
-        lax.fori_loop(0, PAIRS // 4, pick_cells, 0)
+        lax.fori_loop(0, PAIRS // 8, pick_cells, 0)
 
     def gap():
         sort_slots()
@@ -489,8 +489,8 @@
     observe_rows(INNER_FIRST[6:])
 
     def observe(i, carry):
-        for u in range(8):
-            p = 8 * i + u
+        for u in range(14):
+            p = 14 * i + u
             picked = mm(xs[pair_ref[1, p]], onehot[p])
             product = (picked[:LV] + picked[LV:]) * ps[pair_ref[0, p]]
             val[p] = jnp.sum(product, axis=0, keepdims=True)
@@ -499,7 +499,7 @@
     copies = []
     for n, (begin, end) in enumerate(PARTS):
         lax.fori_loop(begin, end, observe, 0)
-        span = slice(8 * begin, 8 * end)
+        span = slice(14 * begin, 14 * end)
         copies.append([
             band_copy(val.at[span], valr.at[o, span], va_s.at[n, o], va_r.at[n, o], o) for o in range(3)])
 
@@ -515,8 +515,8 @@
         adj[2, y] = by
         adj[3, y] = ay
     def spread(i, before):
-        for u in range(8):
-            p = 8 * i + u
+        for u in range(14):
+            p = 14 * i + u
             c = pair_ref[0, p]
             values = (val[p] + valr[0, p]) + (valr[1, p] + valr[2, p])
             high, low = halves(ps[c] * (values * wgtr[c]))

time: 53.7 us -> 52.4 us (0.976)
  Pallas kernels: 50.5 us -> 49.3 us
    pallas_call x1, Pallas kernels: 50.5 us -> 49.3 us  [shards(): pl.pallas_call(kernel, out_shape=jax.ShapeDtypeStruct(increment.shape, F3...]
where the time goes in v6:
time: 52.4 us; the launch traced here: 52.2 us
  Pallas kernels  49.3 us (94%)
  local copies, waits for them, and re-layouts  2.94 us (6%)
    pallas_call x1, Pallas kernels, shards(): pl.pallas_call(kernel, out_shape=jax.ShapeDtypeStruct(increment.shape, F3...  49.3 us
    unnamed x1, local copies, waits for them, and re-layouts  2.94 us

profile of v6, /device:TPU:0, one launch (start us, length us, event | category | flops | bytes accessed | tf_op | source)
XLA Modules:
  0.0 52.2 jit_solution(12224156395244273761)
XLA Ops:
  0.0 49.3 %shard_map.100 = f32[16,5,8,768]{3,2,1,0:T(8,128)} custom-call(f32[16,5,8,768]{3,2,1,0:T(8,128)} %inc_hbm.1, f32[16,8,768]{2,1,0:T(8,128)} %cx_hbm.1, f32[16,8,768]{2,1,0:T(8,128)} %cy_hbm.1, f32[5,16,16]{2,1,0:T(8,128)} %inv_ref.1, f32[5,16,64]{2,1,0:T(8,128)} %bitcast.4, s32[64,128]{1,0:T(8,128)} %bitcast.5, s32[64,128]{1,0:T(8,128)} %bitcast.6, ...), custom_call_target="tpu_custom_call" | custom-call | tf_op jit(solution)/shard_map/pallas_call | solution.py:578
  49.3 2.9 %copy.12 = f32[16,5,8,768]{3,2,1,0:T(8,128)} copy(f32[16,5,8,768]{3,2,1,0:T(8,128)} %shard_map.100) | data formatting | bytes 3932160
